TPU v7x, 128 devices: a whole 4x4x4 slice. The times are simulated.
128 devices in a mesh: fsdp: 16 (over x, y_hi, core), dp: 8 (over y_lo, z).
Axes of the slice: x: 4, y: 4 (y_hi: 2, y_lo: 2; y = y_hi * 2 + y_lo), z: 4, core: 2. Of those that a mesh axis runs over, the one named last changes fastest.
Arguments:
- codes: int32 [9, 16384], P(None, ('fsdp', 'dp')), may hold values from 0 to 1023
- lengths: int32 [1024], P(('fsdp', 'dp')), may hold values from 1 to 16
- owner: int32 [1024, 1], P(('fsdp', 'dp')), may hold values from 0 to 7; in each aligned block of 8 rows (0 to 7, 8 to 15, ...) at most 2 rows name the same one
- codebook: float32 [9, 1024, 1024], P(None, 'fsdp'), may hold values from -5 to 5
- latent_projection_weight: float32 [1024, 1536], P('fsdp'), may hold values from -0.1875 to 0.1875
- snake_upsample_first: float32 [1536], replicated, may hold values from 0.5 to 4
- upsample_weight_first: float32 [1536, 1536], P('fsdp'), may hold values from -0.15625 to 0.15625
- snake_residual_first: float32 [768], replicated, may hold values from 0.5 to 4
- dilated_weight_first: float32 [7, 768, 768], P(None, 'fsdp'), may hold values from -0.078125 to 0.078125
- mixing_weight_first: float32 [768, 768], P('fsdp'), may hold values from -0.21875 to 0.21875
- snake_upsample_second: float32 [768], replicated, may hold values from 0.5 to 4
- upsample_weight_second: float32 [768, 768], P('fsdp'), may hold values from -0.21875 to 0.21875
- snake_residual_second: float32 [384], replicated, may hold values from 0.5 to 4
- dilated_weight_second: float32 [7, 384, 384], P(None, 'fsdp'), may hold values from -0.125 to 0.125
- mixing_weight_second: float32 [384, 384], P('fsdp'), may hold values from -0.3125 to 0.3125
Outputs:
- decoded: bfloat16 [131072, 384], P(('fsdp', 'dp'))
Inputs may be any that keep to these rules, and one draw needn't show every extreme that they name: Among the slabs of one device no owner appears more than 2 times, and some device sends exactly 2 slabs to one owner.
All inputs are finite; a program needn't handle non-finite values.
Results may differ from a plain program's by a relative error of at most 0.015.
Values may be sent and summed in bfloat16 or wider, within the bound.
A program may use at most 320 MiB of HBM per device.

v0:
```python
import jax
import jax.numpy as jnp
from jax import lax
from jax.sharding import PartitionSpec as P

SLAB = 16
FIRST_DILATION = 3
SECOND_DILATION = 9
MOST = 2


def snake(value, snake_frequency):
    return value + jnp.sin(snake_frequency * value) ** 2 / snake_frequency


def dequantize(codes, codebook):
    table = codebook.astype(jnp.bfloat16)
    quantizer_levels = codebook.shape[0]
    width = codebook.shape[2]
    everyone = lax.all_gather(codes, "fsdp", axis=1, tiled=True)
    rows = codes.shape[1]
    local_codes = codebook.shape[1]
    base = lax.axis_index("fsdp") * local_codes
    columns = lax.iota(jnp.int32, local_codes)
    total = jnp.zeros((rows * lax.axis_size("fsdp"), width), jnp.float32)
    for level in range(quantizer_levels):
        onehot = ((everyone[level] - base)[:, None] == columns[None, :]).astype(jnp.bfloat16)
        total = total + jnp.dot(onehot, table[level], preferred_element_type=jnp.float32)
    return lax.psum_scatter(total, "fsdp", scatter_dimension=0, tiled=True)


def masked(latent, lens):
    place = lax.iota(jnp.int32, latent.shape[0])
    keep = place % SLAB < jnp.repeat(lens, SLAB)
    return jnp.where(keep[:, None], latent.astype(jnp.bfloat16), jnp.zeros((), jnp.bfloat16))


def add_taps(total, piece, padded, dilation_step):
    frames = total.shape[1]
    for tap in range(piece.shape[0]):
        window = padded[:, tap * dilation_step : tap * dilation_step + frames]
        total = total + jnp.einsum(
            "sfc,cd->sfd", window, piece[tap], preferred_element_type=jnp.float32
        )
    return total


def body(
    codes,
    lengths,
    owner,
    codebook,
    latent_projection_weight,
    snake_upsample_first,
    upsample_weight_first,
    snake_residual_first,
    dilated_weight_first,
    mixing_weight_first,
    snake_upsample_second,
    upsample_weight_second,
    snake_residual_second,
    dilated_weight_second,
    mixing_weight_second,
):
    brain_float = jnp.bfloat16
    groups = lax.axis_size("dp")
    count = lengths.shape[0]
    dest = owner[:, 0]
    order = lax.iota(jnp.int32, count)
    earlier = (dest[None, :] == dest[:, None]) & (order[None, :] < order[:, None])
    rank = jnp.sum(earlier.astype(jnp.int32), axis=1)
    slot = dest * MOST + rank
    dispatch = slot[None, :] == lax.iota(jnp.int32, groups * MOST)[:, None]
    routed = dispatch.astype(jnp.int32)
    source = jnp.sum(routed * order[None, :], axis=1)
    valid = jnp.sum(routed, axis=1)
    codes_split = codes.reshape(codes.shape[0], count, SLAB)
    send_codes = jnp.take(codes_split, source, axis=1) * valid[None, :, None]
    send_codes = send_codes.reshape(codes.shape[0], groups, MOST * SLAB)
    send_lens = (jnp.take(lengths, source) * valid).reshape(1, groups, MOST)
    got_codes, got_lens = (
        lax.all_to_all(send_codes, "dp", split_axis=1, concat_axis=1, tiled=True),
        lax.all_to_all(send_lens, "dp", split_axis=1, concat_axis=1, tiled=True),
    )
    latent = dequantize(got_codes.reshape(codes.shape[0], -1), codebook)
    slabs = masked(latent, got_lens.reshape(-1)).reshape(groups * MOST, SLAB, -1)
    shards = (
        latent_projection_weight[None],
        upsample_weight_first[None],
        dilated_weight_first,
        mixing_weight_first[None],
        upsample_weight_second[None],
        dilated_weight_second,
        mixing_weight_second[None],
    )
    shards = tuple((weight.astype(brain_float) for weight in shards))

    def project_latent(values, index, dilation_step):
        half = (shards[index].shape[0] - 1) // 2 * dilation_step
        padded = jnp.pad(values, ((0, 0), (half, half), (0, 0)))
        empty = jnp.zeros(values.shape[:2] + (shards[index].shape[2],), jnp.float32)
        return add_taps(
            empty, lax.all_gather(shards[index], "fsdp", axis=1, tiled=True), padded, dilation_step
        )

    def residual_stack_unit(
        upper_bound, snake_frequency, dilated_tap_index, mixing_tap_index, dilation_step
    ):
        active_frames = snake(upper_bound, snake_frequency).astype(brain_float)
        apply_convolution = project_latent(active_frames, dilated_tap_index, dilation_step)
        second = snake(apply_convolution, snake_frequency).astype(brain_float)
        return upper_bound + project_latent(second, mixing_tap_index, 1)

    slots = slabs.shape[0]
    start = project_latent(slabs, 0, 1)
    lifted_one = snake(start, snake_upsample_first).astype(brain_float)
    upsampled_first = project_latent(lifted_one, 1, 1).reshape(slots, 2 * SLAB, -1)
    decoder_block_first = residual_stack_unit(
        upsampled_first, snake_residual_first, 2, 3, FIRST_DILATION
    )
    lifted_two = snake(decoder_block_first, snake_upsample_second).astype(brain_float)
    upsampled_second = project_latent(lifted_two, 4, 1).reshape(slots, 4 * SLAB, -1)
    decoder_block_second = residual_stack_unit(
        upsampled_second, snake_residual_second, 5, 6, SECOND_DILATION
    ).astype(brain_float)
    return decoder_block_second.reshape(slots * 4 * SLAB, -1)


def solution(mesh):
    return jax.shard_map(
        body,
        mesh=mesh,
        in_specs=(
            P(None, ("fsdp", "dp")),
            P(("fsdp", "dp")),
            P(("fsdp", "dp"), None),
            P(None, "fsdp", None),
            P("fsdp", None),
            P(),
            P("fsdp", None),
            P(),
            P(None, "fsdp", None),
            P("fsdp", None),
            P(),
            P("fsdp", None),
            P(),
            P(None, "fsdp", None),
            P("fsdp", None),
        ),
        out_specs=P(("fsdp", "dp"), None),
        check_vma=False,
    )
```

profile of v0, /device:TPU:1, one launch (start us, length us, event | category | flops | bytes accessed | tf_op | source)
XLA Modules:
  0.0 655.1 jit_solution(5766305190794714518)
XLA Ops:
  10.9 6.9 %all-to-all-start.1 = ((s32[8,1,288]{2,1,0:T(1,128)}), s32[8,1,288]{2,1,0:T(1,128)S(1)}, u32[]{:S(2)}, u32[]{:S(2)}) async-start(s32[8,1,288]{2,1,0:T(1,128)} %reshape.278), calls=%async_computation.1 | async-start | bytes 24576 | tf_op jit(solution)/shard_map/all_to_all | solution.py:82
  24.2 26.6 %all_gather.24 = s32[9,4096]{1,0:T(8,128)S(1)} all-gather(s32[9,256]{1,0:T(8,128)S(1)} %reshape.219), channel_id=1, replica_groups=mesh['fsdp'=16,'dp'=8] {'fsdp'}, dimensions={1}, use_global_device_ids=true | all-gather | bytes 156672 | tf_op jit(solution)/shard_map/all_gather | solution.py:20
  51.0 7.0 %fusion.10 = f32[4096,1024]{1,0:T(8,128)} fusion(s32[4096]{0:T(1024)S(1)} %bitcast.151, bf16[9,64,1024]{2,1,0:T(8,128)(2,1)S(1)} %convert_element_type.94), kind=kOutput, calls=%fused_computation.28 | convolution fusion | flops 537133056 | bytes 16924672 | tf_op jit(solution)/shard_map/dot_general | solution.py:28
  58.0 7.0 %fusion.11 = f32[4096,1024]{1,0:T(8,128)} fusion(s32[4096]{0:T(1024)S(1)} %bitcast.150, bf16[9,64,1024]{2,1,0:T(8,128)(2,1)S(1)} %convert_element_type.94), kind=kOutput, calls=%fused_computation.29 | convolution fusion | flops 537133056 | bytes 16924672 | tf_op jit(solution)/shard_map/dot_general | solution.py:28
  65.0 7.1 %fusion.4 = f32[4096,1024]{1,0:T(8,128)} fusion(s32[4096]{0:T(1024)S(1)} %bitcast.149, bf16[9,64,1024]{2,1,0:T(8,128)(2,1)S(1)} %convert_element_type.94), kind=kOutput, calls=%fused_computation.22 | convolution fusion | flops 537133056 | bytes 16924672 | tf_op jit(solution)/shard_map/dot_general | solution.py:28
  72.2 7.0 %fusion.5 = f32[4096,1024]{1,0:T(8,128)} fusion(s32[4096]{0:T(1024)S(1)} %bitcast.148, bf16[9,64,1024]{2,1,0:T(8,128)(2,1)S(1)} %convert_element_type.94), kind=kOutput, calls=%fused_computation.23 | convolution fusion | flops 537133056 | bytes 16924672 | tf_op jit(solution)/shard_map/dot_general | solution.py:28
  79.2 7.1 %fusion.6 = f32[4096,1024]{1,0:T(8,128)} fusion(s32[4096]{0:T(1024)S(1)} %bitcast.147, bf16[9,64,1024]{2,1,0:T(8,128)(2,1)S(1)} %convert_element_type.94), kind=kOutput, calls=%fused_computation.24 | convolution fusion | flops 537133056 | bytes 16924672 | tf_op jit(solution)/shard_map/dot_general | solution.py:28
  86.3 7.0 %fusion.7 = f32[4096,1024]{1,0:T(8,128)} fusion(s32[4096]{0:T(1024)S(1)} %bitcast.146, bf16[9,64,1024]{2,1,0:T(8,128)(2,1)S(1)} %convert_element_type.94), kind=kOutput, calls=%fused_computation.25 | convolution fusion | flops 537133056 | bytes 16924672 | tf_op jit(solution)/shard_map/dot_general | solution.py:28
  93.3 7.0 %fusion.8 = f32[4096,1024]{1,0:T(8,128)} fusion(s32[4096]{0:T(1024)S(1)} %bitcast.145, bf16[9,64,1024]{2,1,0:T(8,128)(2,1)S(1)} %convert_element_type.94), kind=kOutput, calls=%fused_computation.26 | convolution fusion | flops 537133056 | bytes 16924672 | tf_op jit(solution)/shard_map/dot_general | solution.py:28
  100.3 7.0 %fusion.9 = f32[4096,1024]{1,0:T(8,128)} fusion(s32[4096]{0:T(1024)S(1)} %bitcast.144, bf16[9,64,1024]{2,1,0:T(8,128)(2,1)S(1)} %convert_element_type.94), kind=kOutput, calls=%fused_computation.27 | convolution fusion | flops 537133056 | bytes 16924672 | tf_op jit(solution)/shard_map/dot_general | solution.py:28
  107.4 47.4 %add_add_fusion = f32[4096,1024]{1,0:T(8,128)} fusion(f32[4096,1024]{1,0:T(8,128)} %fusion.11, f32[4096,1024]{1,0:T(8,128)} %fusion.10, f32[4096,1024]{1,0:T(8,128)} %fusion.9, f32[4096,1024]{1,0:T(8,128)} %fusion.8, f32[4096,1024]{1,0:T(8,128)} %fusion.7, f32[4096,1024]{1,0:T(8,128)} %fusion.6, f32[4096,1024]{1,0:T(8,128)} %fusion.4, ...), kind=kOutput, calls=%fused_computation.2 | convolution fusion | flops 570687488 | bytes 151142400 | tf_op jit(solution)/shard_map/dot_general | solution.py:28
  165.4 20.3 %all-gather.4 = bf16[384,384]{1,0:T(8,128)(2,1)S(1)} all-gather(bf16[24,384]{1,0:T(8,128)(2,1)S(1)} %convert_element_type.116), channel_id=6, replica_groups=mesh['fsdp'=16,'dp'=8] {'fsdp'}, dimensions={0}, use_global_device_ids=true | all-gather | bytes 313344 | tf_op jit(solution)/shard_map/all_gather | solution.py:103
  187.1 108.5 %reduce-scatter.2.cloned.1.call-done = f32[256,1024]{1,0:T(8,128)} async-done(((f32[4096,1024]{1,0:T(8,128)}), f32[256,1024]{1,0:T(8,128)}) %reduce-scatter.2.cloned.1.call-update) | async-done | bytes 1048592 | tf_op jit(solution)/shard_map/reduce_scatter | solution.py:29
  297.0 52.4 %all-gather.16.cloned.1.call-done = bf16[1024,1536]{1,0:T(8,128)(2,1)} async-done(((bf16[64,1536]{1,0:T(8,128)(2,1)}), bf16[1024,1536]{1,0:T(8,128)(2,1)}) %all-gather.16.cloned.1.call-update) | async-done | bytes 3145744 | tf_op jit(solution)/shard_map/all_gather | solution.py:103
  349.4 59.4 %all-gather.18.cloned.1.call-done = bf16[1536,1536]{1,0:T(8,128)(2,1)} async-done(((bf16[96,1536]{1,0:T(8,128)(2,1)}), bf16[1536,1536]{1,0:T(8,128)(2,1)}) %all-gather.18.cloned.1.call-update) | async-done | bytes 4718608 | tf_op jit(solution)/shard_map/all_gather | solution.py:103
  408.8 16.5 %add_convert_fusion.6 = (bf16[16,16,1536]{2,1,0:T(8,128)(2,1)}, f32[16,16,1536]{2,1,0:T(8,128)S(1)}) fusion(f32[1536]{0:T(1024)S(1)} %mul.120, bf16[1536,1536]{1,0:T(8,128)(2,1)} %all-gather.18.cloned.1.call-done, bf16[16,16,1024]{2,1,0:T(8,128)(2,1)S(1)} %bitcast.140, bf16[1024,1536]{1,0:T(8,128)(2,1)} %all-gather.16.cloned.1.call-done, ...), kind=kOutput, calls=%fused_computation.42 | convolution fusion | flops 2017198080 | bytes 10760192 | tf_op jit(solution)/shard_map/sfc,cd->sfd/dot_general | solution.py:42
  432.3 50.1 %all-gather.12.cloned.1.call-done = bf16[7,768,768]{2,1,0:T(8,128)(2,1)} async-done(((bf16[7,48,768]{2,1,0:T(8,128)(2,1)}), bf16[7,768,768]{2,1,0:T(8,128)(2,1)}) %all-gather.12.cloned.1.call-update) | async-done | bytes 8257552 | tf_op jit(solution)/shard_map/all_gather | solution.py:103
  491.7 7.0 %add_convert_fusion.5 = bf16[16,32,768]{2,1,0:T(8,128)(2,1)} fusion(f32[16,32,768]{2,1,0:T(8,128)S(1)} %fusion.15, f32[16,32,768]{2,1,0:T(8,128)S(1)} %fusion.16, f32[16,32,768]{2,1,0:T(8,128)S(1)} %fusion.17, f32[16,32,768]{2,1,0:T(8,128)S(1)} %fusion.18, f32[16,32,768]{2,1,0:T(8,128)S(1)} %fusion.20, f32[16,32,768]{2,1,0:T(8,128)S(1)} %fusion.19, ...), kind=kOutput, calls=%fused_computation.41 | convolution fusion | flops 608305152 | bytes 12193792 | tf_op jit(solution)/shard_map/sfc,cd->sfd/dot_general | solution.py:42
  498.7 29.6 %all-gather.20.cloned.1.call-done = bf16[768,768]{1,0:T(8,128)(2,1)} async-done(((bf16[48,768]{1,0:T(8,128)(2,1)}), bf16[768,768]{1,0:T(8,128)(2,1)}) %all-gather.20.cloned.1.call-update) | async-done | bytes 1179664 | tf_op jit(solution)/shard_map/all_gather | solution.py:103
  528.3 46.8 %all-gather.22.cloned.1.call-done = bf16[768,768]{1,0:T(8,128)(2,1)} async-done(((bf16[48,768]{1,0:T(8,128)(2,1)}), bf16[768,768]{1,0:T(8,128)(2,1)}) %all-gather.22.cloned.1.call-update) | async-done | bytes 1179664 | tf_op jit(solution)/shard_map/all_gather | solution.py:103
  575.1 14.2 %add_convert_fusion.2 = (bf16[16,32,768]{2,1,0:T(8,128)(2,1)}, f32[16,32,768]{2,1,0:T(8,128)}) fusion(f32[768]{0:T(1024)S(1)} %mul.129, bf16[768,768]{1,0:T(8,128)(2,1)} %all-gather.22.cloned.1.call-done, f32[16,32,768]{2,1,0:T(8,128)S(1)} %reshape.221, bf16[16,32,768]{2,1,0:T(8,128)(2,1)} %add_convert_fusion.5, ...), kind=kOutput, calls=%fused_computation.38 | convolution fusion | flops 1212284928 | bytes 7084032 | tf_op jit(solution)/shard_map/sfc,cd->sfd/dot_general | solution.py:42
  591.3 5.6 add_convert_fusion.3
  596.8 27.9 %all-gather.14.cloned.1.call-done = bf16[7,384,384]{2,1,0:T(8,128)(2,1)} async-done(((bf16[7,24,384]{2,1,0:T(8,128)(2,1)}), bf16[7,384,384]{2,1,0:T(8,128)(2,1)}) %all-gather.14.cloned.1.call-update) | async-done | bytes 2064400 | tf_op jit(solution)/shard_map/all_gather | solution.py:103
  636.8 11.1 %add_convert_fusion = bf16[16,64,384]{2,1,0:T(8,128)(2,1)} fusion(f32[16,64,384]{2,1,0:T(8,128)S(1)} %reshape.222, f32[16,64,384]{2,1,0:T(8,128)} %fusion.39, f32[16,64,384]{2,1,0:T(8,128)} %fusion.38, f32[16,64,384]{2,1,0:T(8,128)} %fusion.43, f32[16,64,384]{2,1,0:T(8,128)} %fusion.37, f32[16,64,384]{2,1,0:T(8,128)} %fusion.35, ...), kind=kOutput, calls=%fused_computation.36 | convolution fusion | flops 609091584 | bytes 13174272 | tf_op jit(solution)/shard_map/sfc,cd->sfd/dot_general | solution.py:42
  (114 shorter events, 54.1 us)
Async XLA Ops:
  6.5 153.4 %copy-start = (s32[8]{0:T(128)S(1)}, s32[8]{0:T(128)}, u32[]{:S(2)}) copy-start(s32[8]{0:T(128)} %param.16) | copy-start | bytes 100
  10.9 11.9 %all-to-all-start.1 = ((s32[8,1,288]{2,1,0:T(1,128)}), s32[8,1,288]{2,1,0:T(1,128)S(1)}, u32[]{:S(2)}, u32[]{:S(2)}) async-start(s32[8,1,288]{2,1,0:T(1,128)} %reshape.278), calls=%async_computation.1 | async-start | bytes 24576 | tf_op jit(solution)/shard_map/all_to_all | solution.py:82
  17.8 277.8 %reduce-scatter.2.cloned.1.call-start = ((), (), s32[]{:S(2)}) async-start(), calls=%async_computation.3 | async-start | bytes 17825792 | tf_op jit(solution)/shard_map/reduce_scatter | solution.py:29
  154.7 1.0 copy-start.5
  154.7 1.8 copy-start.4
  154.8 2.7 copy-start.2
  154.8 194.6 %all-gather.16.cloned.1.call-start = ((), (), s32[]{:S(2)}) async-start(), calls=%async_computation.6 | async-start | bytes 3342336 | tf_op jit(solution)/shard_map/all_gather | solution.py:103
  156.5 1.9 copy-start.7
  156.5 2.6 copy-start.8
  156.5 252.3 %all-gather.18.cloned.1.call-start = ((), (), s32[]{:S(2)}) async-start(), calls=%async_computation.7 | async-start | bytes 5013504 | tf_op jit(solution)/shard_map/all_gather | solution.py:103
  157.3 7.3 %copy-start.6 = (f32[7,24,384]{2,1,0:T(8,128)S(1)}, f32[7,24,384]{2,1,0:T(8,128)}, u32[]{:S(2)}) copy-start(f32[7,24,384]{2,1,0:T(8,128)} %param.28) | copy-start | bytes 774148
  157.3 8.0 %copy-start.11 = (f32[768]{0:T(1024)S(1)}, f32[768]{0:T(1024)}, u32[]{:S(2)}) copy-start(f32[768]{0:T(1024)} %param.22) | copy-start | bytes 9220
  157.4 8.0 %copy-start.9 = (f32[24,384]{1,0:T(8,128)S(1)}, f32[24,384]{1,0:T(8,128)}, u32[]{:S(2)}) copy-start(f32[24,384]{1,0:T(8,128)} %param.29) | copy-start | bytes 110596
  157.4 325.0 %all-gather.12.cloned.1.call-start = ((), (), s32[]{:S(2)}) async-start(), calls=%async_computation.4 | async-start | bytes 8773632 | tf_op jit(solution)/shard_map/all_gather | solution.py:103
  158.3 27.4 %copy-start.10 = (f32[384]{0:T(512)S(1)}, f32[384]{0:T(512)}, u32[]{:S(2)}) copy-start(f32[384]{0:T(512)} %param.27) | copy-start | bytes 4612
  158.3 370.0 %all-gather.20.cloned.1.call-start = ((), (), s32[]{:S(2)}) async-start(), calls=%async_computation.8 | async-start | bytes 1253376 | tf_op jit(solution)/shard_map/all_gather | solution.py:103
  159.0 416.1 %all-gather.22.cloned.1.call-start = ((), (), s32[]{:S(2)}) async-start(), calls=%async_computation.9 | async-start | bytes 1253376 | tf_op jit(solution)/shard_map/all_gather | solution.py:103
  159.7 249.1 %copy-start.13 = (f32[1536]{0:T(1024)S(1)}, f32[1536]{0:T(1024)}, u32[]{:S(2)}) copy-start(f32[1536]{0:T(1024)} %param.20) | copy-start | bytes 18436
  161.3 24.4 %all-to-all-start = ((s32[1,8,2]{2,0,1:T(1,128)}), s32[1,8,2]{2,0,1:T(1,128)S(1)}, u32[]{:S(2)}, u32[]{:S(2)}) async-start(s32[1,8,2]{2,0,1:T(1,128)} %bitcast.3), calls=%async_computation | async-start | bytes 8192 | tf_op jit(solution)/shard_map/all_to_all | solution.py:83
  164.6 460.2 %all-gather.14.cloned.1.call-start = ((), (), s32[]{:S(2)}) async-start(), calls=%async_computation.5 | async-start | bytes 2193408 | tf_op jit(solution)/shard_map/all_gather | solution.py:103
  482.4 6.8 %copy-start.12 = (bf16[7,768,768]{2,1,0:T(8,128)(2,1)S(1)}, bf16[7,768,768]{2,1,0:T(8,128)(2,1)}, u32[]{:S(2)}) copy-start(bf16[7,768,768]{2,1,0:T(8,128)(2,1)} %all-gather.12.cloned.1.call-done) | copy-start | bytes 24772612
  491.7 83.5 %copy-start.14 = (f32[768]{0:T(1024)S(1)}, f32[768]{0:T(1024)}, u32[]{:S(2)}) copy-start(f32[768]{0:T(1024)} %param.25) | copy-start | bytes 9220
  589.4 1.6 copy-start.3
  624.8 2.9 copy-start.1
Sparse Core Ops, SparseCore 0:
  154.9 140.6 reduce-scatter.1
  298.3 51.0 all-gather.15
  352.1 56.6 all-gather.17
  411.4 70.9 all-gather.11
  484.9 43.3 all-gather.19
  530.9 44.2 all-gather.21
  577.7 47.0 all-gather.13
where the time goes:
time: 665 us; the launch traced here: 655 us
  waiting for transfers between devices  378 us (57%)
  matrix products  174 us (26%)
  blocking collectives  46.9 us (7%)
  other arithmetic  22.2 us (3%)
  between operations  14.3 us (2%)
  starting transfers between devices  10.4 us (2%)
  local copies, waits for them, and re-layouts  9.43 us (1%)
    all_gather x6, waiting for transfers between devices, project_latent(): lax.all_gather(shards[index], 'fsdp', axis=1, tiled=True)  266 us
    reduce_scatter x1, waiting for transfers between devices, dequantize(): return lax.psum_scatter(total, 'fsdp', scatter_dimension=0, tiled=True)  108 us
    dot_general x9, matrix products, dequantize(): jnp.dot(onehot, table[level], preferred_element_type=jnp.float32)  104 us
    dot_general x16, matrix products, add_taps(): jnp.einsum('sfc,cd->sfd', window, piece[tap], preferred_element_type=jnp....  70.1 us
    all_gather x1, blocking collectives, dequantize(): everyone = lax.all_gather(codes, 'fsdp', axis=1, tiled=True)  26.6 us
    all_gather x1, blocking collectives, project_latent(): lax.all_gather(shards[index], 'fsdp', axis=1, tiled=True)  20.3 us
  transfers between devices with their start and end apart: 9, of which 8 were waited for; matrix products, arithmetic and copies ran while one was open for 11% of the time, Pallas kernels for 0%

commit v1 on v0

v1 whole, which is shorter than its diff:
```python
import jax
import jax.numpy as jnp
from jax import lax
from jax.experimental import pallas as pl
from jax.experimental.pallas import tpu as pltpu
from jax.sharding import PartitionSpec as P

SLAB = 16
MOST = 2
BF = jnp.bfloat16
F32 = jnp.float32
POLY = (
    9.869604311819561,
    -32.46967117891694,
    42.72719645855932,
    -30.101466599015037,
    13.05010051862992,
    -3.3565928630444257,
)
INV_PI = 0.3183098861837907
PAD1 = 8
PAD2 = 26


def snake(value, freq):
    turns = value * (freq * INV_PI)
    frac = turns - jnp.round(turns)
    u = frac * frac
    poly = jnp.full_like(u, POLY[-1])
    for coef in POLY[-2::-1]:
        poly = poly * u + coef
    return value + (poly * u) * (1.0 / freq)


def dot(left, right):
    return jnp.dot(left, right, preferred_element_type=F32)


class Links:
    def __init__(self, send_sems, recv_sems):
        self.send_sems, self.recv_sems, self.used, self.sent = send_sems, recv_sems, 0, []

    def new(self):
        self.used += 1
        return self.used - 1

    def copy(self, src, dst, dev, number):
        return pltpu.make_async_remote_copy(
            src_ref=src,
            dst_ref=dst,
            send_sem=self.send_sems.at[number],
            recv_sem=self.recv_sems.at[number],
            device_id=dev,
            device_id_type=pl.DeviceIdType.MESH,
        )

    def send(self, src, dev, number, dst=None):
        copy = self.copy(src, src if dst is None else dst, dev, number)
        copy.start()
        self.sent.append(copy)

    def wait(self, region, dev, number):
        self.copy(region, region, dev, number).wait_recv()


def kernel(
    codes_ref, src_ref, cb_hbm, w0_hbm, w1_hbm, w23_hbm, w4_hbm, w56_hbm, a0_ref, a1_ref, a2_ref, a3_ref,
    out_ref,
    codes_all, cbf, w0f, w1f, w23f, w4f, s56, table, onehot,
    fwd_out, fwd_in, far_out, far_in, sum_out, sum_in, keep, ypart_out, ypart_in,
    w0b, w1b, w23b, w4b, w56b,
    lat, lift1, up1, act_a1, act_b1, acc1, sec1, lift2, up2, act_a2, act_b2, sec2, block2, outbuf,
    send_sems, recv_sems, local_sems,
):
    f = lax.axis_index("fsdp")
    d = lax.axis_index("dp")
    x, yh, c = lax.div(f, 4), lax.rem(lax.div(f, 2), 2), lax.rem(f, 2)
    yl, z = lax.div(d, 4), lax.rem(d, 4)
    g = x * 2 + yh

    def dev(x_, yh_, yl_, z_, c_):
        return {"fsdp": (x_ * 2 + yh_) * 2 + c_, "dp": yl_ * 4 + z_}

    def plus(value, step):
        return lax.rem(value + step, 4)

    xp, xm, x2 = plus(x, 1), plus(x, 3), plus(x, 2)
    zp, zm, z2 = plus(z, 1), plus(z, 3), plus(z, 2)
    xs, xr = plus(x, 1 + 2 * c), plus(x, 3 + 2 * c)
    oyh = 1 - yh

    def at_x(xt):
        return dev(xt, yh, yl, z, c)

    def at_z(zt):
        return dev(x, yh, yl, zt, c)

    at_y = dev(x, oyh, 1 - yl, z, c)
    sib = dev(x, yh, yl, z, 1 - c)
    links = Links(send_sems, recv_sems)
    local_count = [0]

    def load(src, dst):
        copy = pltpu.make_async_copy(src, dst, local_sems.at[local_count[0]])
        local_count[0] += 1
        copy.start()
        return copy

    zcols = pl.ds(pl.multiple_of(z * 384, 384), 384)
    ld_cb = load(cb_hbm, cbf)
    ld_w1 = load(w1_hbm.at[:, zcols], w1f)
    ld_w23 = load(w23_hbm.at[pl.ds(2 * z, 2)], w23f)
    ld_w0 = load(w0_hbm, w0f)
    ld_w4 = load(w4_hbm, w4f)
    own24 = pl.ds(pl.multiple_of(c * 24, 8), 24)
    ld_w56 = load(w56_hbm.at[pl.ds(4 * c, 4)], s56.at[:, own24])
    codes_all[x, yh] = codes_ref[...]

    mates = []
    for step in range(4):
        if step:
            mates.append(at_x(plus(x, step)))
        mates.append(dev(plus(x, step), oyh, 1 - yl, z, c))
    owners = [lax.rem(d + step, 8) for step in range(1, 8)]
    barrier = pltpu.get_barrier_semaphore()
    peers = mates + [sib] + [{"fsdp": f, "dp": o} for o in owners]
    for peer in peers:
        pl.semaphore_signal(barrier, inc=1, device_id=peer, device_id_type=pl.DeviceIdType.MESH)
    pl.semaphore_wait(barrier, len(peers))

    code_ids = [links.new() for _ in mates]
    for number, mate in zip(code_ids, mates):
        links.send(codes_all.at[x, yh], mate, number)
    id_56 = links.new()
    links.send(w56_hbm.at[pl.ds(4 * (1 - c), 4)], sib, id_56, dst=s56.at[:, own24])

    ld_cb.wait()
    own64 = pl.ds(pl.multiple_of(c * 64, 64), 64)
    oth64 = pl.ds(pl.multiple_of((1 - c) * 64, 64), 64)
    for level in range(9):
        table[level, own64, :] = cbf[level].astype(BF)
    id_table = links.new()
    links.send(table.at[:, own64], sib, id_table)

    class Quarter:
        def __init__(self, block, row, full, half):
            self.block, self.row, self.full, self.half = block, row, full, half
            self.ids = [links.new() for _ in range(12)]

        def start(self):
            for number, xt in zip(self.ids[:3], (xp, xm, x2)):
                links.send(self.block(z, x, yh), at_x(xt), number)

        def to_y(self):
            for number, xt in zip(self.ids[:3], (xm, xp, x2)):
                links.wait(self.block(z, xt, yh), at_x(xt), number)
            links.send(self.row(z, yh), at_y, self.ids[3])

        def to_z(self):
            links.wait(self.row(z, oyh), at_y, self.ids[3])
            links.send(self.full(z), at_z(zp), self.ids[4])
            links.send(self.full(z), at_z(zm), self.ids[5])
            links.send(self.full(z), sib, self.ids[8])

        def pass_z(self):
            links.wait(self.full(zm), at_z(zm), self.ids[4])
            links.send(self.half(zm, 0), at_z(zp), self.ids[6])
            links.wait(self.full(zp), at_z(zp), self.ids[5])
            links.send(self.half(zp, 1), at_z(zm), self.ids[7])
            links.send(self.full(zm), sib, self.ids[9])
            links.send(self.full(zp), sib, self.ids[10])

        def finish(self):
            links.wait(self.half(z2, 0), at_z(zm), self.ids[6])
            links.wait(self.half(z2, 1), at_z(zp), self.ids[7])
            links.send(self.full(z2), sib, self.ids[11])

        def done(self):
            for number in self.ids[8:]:
                links.wait(self.full(z), sib, number)

    class Plain:
        def __init__(self, block, pair):
            self.block, self.pair = block, pair
            self.ids = [links.new() for _ in range(9)]

        def start(self):
            links.send(self.block(x, yh), at_y, self.ids[0])

        def to_x(self):
            links.wait(self.block(x, oyh), at_y, self.ids[0])
            links.send(self.pair(x), at_x(xp), self.ids[1])
            links.send(self.pair(x), at_x(xm), self.ids[2])
            links.send(self.pair(x), sib, self.ids[5])

        def pass_x(self):
            links.wait(self.pair(xm), at_x(xm), self.ids[1])
            links.send(self.block(xm, 0), at_x(xp), self.ids[3])
            links.wait(self.pair(xp), at_x(xp), self.ids[2])
            links.send(self.block(xp, 1), at_x(xm), self.ids[4])
            links.send(self.pair(xm), sib, self.ids[6])
            links.send(self.pair(xp), sib, self.ids[7])

        def finish(self):
            links.wait(self.block(x2, 0), at_x(xm), self.ids[3])
            links.wait(self.block(x2, 1), at_x(xp), self.ids[4])
            links.send(self.pair(x2), sib, self.ids[8])

        def done(self):
            for number in self.ids[5:]:
                links.wait(self.pair(x), sib, number)

    def columns(zt):
        return pl.ds(pl.multiple_of(zt * 384, 384), 384)

    q1 = Quarter(
        lambda zt, xt, yt: w1b.at[xt, yt, c, :, columns(zt)],
        lambda zt, yt: w1b.at[:, yt, c, :, columns(zt)],
        lambda zt: w1b.at[:, :, c, :, columns(zt)],
        lambda zt, h: w1b.at[:, h, c, :, columns(zt)],
    )

    def tap_quarter(odd):
        return Quarter(
            lambda zt, xt, yt: w23b.at[2 * zt + odd, xt, yt, c],
            lambda zt, yt: w23b.at[2 * zt + odd, :, yt, c],
            lambda zt: w23b.at[2 * zt + odd, :, :, c],
            lambda zt, h: w23b.at[2 * zt + odd, :, h, c],
        )

    qa, qb = tap_quarter(0), tap_quarter(1)
    p0 = Plain(lambda xt, yt: w0b.at[xt, yt, c], lambda xt: w0b.at[xt, :, c])
    p4 = Plain(lambda xt, yt: w4b.at[xt, yt, c], lambda xt: w4b.at[xt, :, c])
    p56 = Plain(lambda xt, yt: w56b.at[c, :, xt, yt], lambda xt: w56b.at[c, :, xt])

    ld_w1.wait()
    w1b[x, yh, c, :, zcols] = w1f[...].astype(BF)
    q1.start()
    ld_w0.wait()
    w0b[x, yh, c] = w0f[...].astype(BF)
    p0.start()
    ld_w23.wait()
    w23b[2 * z, x, yh, c] = w23f[0].astype(BF)
    qa.start()
    w23b[2 * z + 1, x, yh, c] = w23f[1].astype(BF)
    qb.start()
    ld_w4.wait()
    w4b[x, yh, c] = w4f[...].astype(BF)
    p4.start()
    ld_w56.wait()
    links.wait(s56.at[:, own24], sib, id_56)
    for tap in range(4):
        w56b[c, tap, x, yh] = s56[tap].astype(BF)
    p56.start()

    for number, mate in zip(code_ids, mates):
        links.wait(codes_all.at[x, yh], mate, number)
    links.wait(table.at[:, oth64], sib, id_table)

    def partial(xt, put):
        place = lax.broadcasted_iota(jnp.int32, (128, 128), 0) + g * 128
        for yt in range(2):
            codes = codes_all[xt, yt]
            for level in range(9):
                hit = codes[level : level + 1, :] == place
                onehot[pl.ds(level * 128, 128), pl.ds(yt * 128, 128)] = jnp.where(hit, 1.0, 0.0).astype(BF)

        def tile(n, carry):
            cols = pl.ds(pl.multiple_of(n * 256, 256), 256)
            rows = table[:, :, cols].reshape(1152, 256)
            total = lax.dot_general(onehot[...], rows, (((0,), (0,)), ((), ())), preferred_element_type=F32)
            put(cols, total)
            return carry

        lax.fori_loop(0, 4, tile, 0)

    def into(ref):
        def put(cols, total):
            ref[:, cols] = total.astype(ref.dtype)

        return put

    id_fwd, id_far, id_sum, id_y = (links.new() for _ in range(4))
    partial(x2, into(fwd_out))
    links.send(fwd_out, at_x(xs), id_fwd, dst=fwd_in)
    q1.to_y()
    p0.to_x()
    partial(xr, into(far_out))
    links.send(far_out, at_x(xr), id_far, dst=far_in)
    qa.to_y()
    partial(xs, into(keep))
    links.wait(fwd_in, at_x(xr), id_fwd)
    sum_out[...] = (keep[...] + fwd_in[...].astype(F32)).astype(BF)
    links.send(sum_out, at_x(xs), id_sum, dst=sum_in)
    q1.to_z()
    qb.to_y()
    partial(x, into(keep))
    qa.to_z()
    p4.to_x()
    p56.to_x()
    p0.pass_x()
    links.wait(far_in, at_x(xs), id_far)
    links.wait(sum_in, at_x(xr), id_sum)
    keep[...] += far_in[...].astype(F32) + sum_in[...].astype(F32)
    mine = pl.ds(pl.multiple_of(yh * 128, 128), 128)
    theirs = pl.ds(pl.multiple_of(oyh * 128, 128), 128)
    ypart_out[...] = keep[theirs, :].astype(BF)
    links.send(ypart_out, at_y, id_y, dst=ypart_in)
    qb.to_z()
    q1.pass_z()
    p0.finish()
    links.wait(ypart_in, at_y, id_y)
    lat[...] = (keep[mine, :] + ypart_in[...].astype(F32)).astype(BF)
    p0.done()

    def start_tile(n, carry):
        cols = pl.ds(pl.multiple_of(n * 256, 256), 256)
        total = dot(lat[...], w0b[:, :, :, :, cols].reshape(1024, 256))
        lift1[:, cols] = snake(total, a0_ref[:, cols]).astype(BF)
        return carry

    lax.fori_loop(0, 6, start_tile, 0)
    qa.pass_z()
    q1.finish()
    p4.pass_x()
    p56.pass_x()
    q1.done()

    def up1_tile(n, carry):
        cols = pl.ds(pl.multiple_of(n * 256, 256), 256)
        total = dot(lift1[...], w1b[:, :, :, :, cols].reshape(1536, 256))
        phase, part = lax.div(n, 3), lax.rem(n, 3)
        up1[:, phase, :, pl.ds(pl.multiple_of(part * 256, 256), 256)] = total.reshape(16, 8, 256)
        return carry

    lax.fori_loop(0, 6, up1_tile, 0)
    qb.pass_z()
    qa.finish()
    p4.finish()
    p56.finish()

    act_a1[pl.ds(0, 8 * PAD1), :] = jnp.zeros((8 * PAD1, 768), BF)
    act_a1[pl.ds(8 * (PAD1 + 32), 8 * PAD1), :] = jnp.zeros((8 * PAD1, 768), BF)
    act_b1[pl.ds(0, 8 * PAD1), :] = jnp.zeros((8 * PAD1, 768), BF)
    act_b1[pl.ds(8 * (PAD1 + 34), 8 * PAD1), :] = jnp.zeros((8 * PAD1, 768), BF)

    def act1_tile(n, carry):
        cols = pl.ds(pl.multiple_of(n * 256, 256), 256)
        act = snake(up1[:, :, :, cols].reshape(256, 256), a1_ref[:, cols])
        edge = jnp.zeros((8, 256), F32)
        act_a1[pl.ds(8 * PAD1, 256), cols] = act.astype(BF)
        act_b1[pl.ds(8 * PAD1, 272), cols] = jnp.concatenate([edge, act, edge], axis=0).astype(BF)
        return carry

    lax.fori_loop(0, 3, act1_tile, 0)
    qa.done()

    def conv1_tile(taps, n):
        cols = pl.ds(pl.multiple_of(n * 256, 256), 256)
        total = None
        for tap in taps:
            shift = 3 * (tap - 3)
            if shift % 2:
                window = act_b1[pl.ds(8 * (PAD1 + 1 + shift), 256), :]
            else:
                window = act_a1[pl.ds(8 * (PAD1 + shift), 256), :]
            term = dot(window, w23b[tap, :, :, :, :, cols].reshape(768, 256))
            total = term if total is None else total + term
        return cols, total

    def conv1_even(n, carry):
        cols, total = conv1_tile((0, 2, 4, 6), n)
        acc1[:, cols] = total
        return carry

    def conv1_odd(n, carry):
        cols, total = conv1_tile((1, 3, 5), n)
        sec1[:, cols] = snake(acc1[:, cols] + total, a1_ref[:, cols]).astype(BF)
        return carry

    lax.fori_loop(0, 3, conv1_even, 0)
    qb.finish()
    qb.done()
    lax.fori_loop(0, 3, conv1_odd, 0)

    def mix1_tile(n, carry):
        cols = pl.ds(pl.multiple_of(n * 256, 256), 256)
        total = dot(sec1[...], w23b[7, :, :, :, :, cols].reshape(768, 256))
        block = up1[:, :, :, cols].reshape(256, 256) + total
        lift2[:, cols] = snake(block, a2_ref[:, cols]).astype(BF)
        return carry

    lax.fori_loop(0, 3, mix1_tile, 0)
    p4.done()

    def up2_tile(n, carry):
        rows = pl.ds(pl.multiple_of(n * 64, 64), 64)
        total = dot(lift2[rows, :], w4b[...].reshape(768, 768))
        for phase in range(2):
            up2[pl.ds(n * 8, 8), phase] = total[:, phase * 384 : (phase + 1) * 384].reshape(8, 8, 384)
        return carry

    lax.fori_loop(0, 4, up2_tile, 0)

    act_a2[pl.ds(0, 8 * PAD2), :] = jnp.zeros((8 * PAD2, 384), BF)
    act_a2[pl.ds(8 * (PAD2 + 64), 8 * PAD2), :] = jnp.zeros((8 * PAD2, 384), BF)
    act_b2[pl.ds(0, 8 * PAD2), :] = jnp.zeros((8 * PAD2, 384), BF)
    act_b2[pl.ds(8 * (PAD2 + 66), 8 * PAD2), :] = jnp.zeros((8 * PAD2, 384), BF)

    def act2_tile(n, carry):
        cols = pl.ds(pl.multiple_of(n * 128, 128), 128)
        act = snake(up2[:, :, :, cols].reshape(512, 128), a3_ref[:, cols])
        edge = jnp.zeros((8, 128), F32)
        act_a2[pl.ds(8 * PAD2, 512), cols] = act.astype(BF)
        act_b2[pl.ds(8 * PAD2, 528), cols] = jnp.concatenate([edge, act, edge], axis=0).astype(BF)
        return carry

    lax.fori_loop(0, 3, act2_tile, 0)
    p56.done()

    def conv2_tile(n, carry):
        start = n * 128
        total = None
        for tap in range(7):
            shift = 9 * (tap - 3)
            if shift % 2:
                window = act_b2[pl.ds(pl.multiple_of(8 * (PAD2 + 1 + shift) + start, 16), 128), :]
            else:
                window = act_a2[pl.ds(pl.multiple_of(8 * (PAD2 + shift) + start, 16), 128), :]
            term = dot(window, w56b[tap // 4, tap % 4].reshape(384, 384))
            total = term if total is None else total + term
        second = snake(total, a3_ref[...]).astype(BF)
        block = up2[pl.ds(n * 8, 8)].reshape(128, 384) + dot(second, w56b[1, 3].reshape(384, 384))
        block2[pl.ds(pl.multiple_of(start, 128), 128), :] = block.astype(BF)
        return carry

    lax.fori_loop(0, 4, conv2_tile, 0)

    gap = lax.broadcasted_iota(jnp.int32, (64, 512), 1) - 8 * lax.broadcasted_iota(jnp.int32, (64, 512), 0)
    for owner in range(8):
        pick = jnp.concatenate(
            [jnp.where(gap == src_ref[owner * MOST + r], 1.0, 0.0).astype(BF) for r in range(MOST)], axis=0
        )
        outbuf[owner] = dot(pick, block2[...]).astype(BF)
    out_ids = [links.new() for _ in owners]
    here = pl.ds(pl.multiple_of(d * 128, 128), 128)
    for number, o in zip(out_ids, owners):
        links.send(outbuf.at[o], {"fsdp": f, "dp": o}, number, dst=out_ref.at[here])
    out_ref[here, :] = outbuf[d]
    for number in out_ids:
        links.wait(out_ref.at[here], sib, number)
    for copy in links.sent:
        copy.wait_send()


def body(codes, lengths, owner, codebook, w0, a0, w1, a1, w2, w3, a2, w4, a3, w5, w6):
    count = lengths.shape[0]
    dest = owner[:, 0]
    order = lax.iota(jnp.int32, count)
    earlier = (dest[None, :] == dest[:, None]) & (order[None, :] < order[:, None])
    rank = jnp.sum(earlier.astype(jnp.int32), axis=1)
    slot = dest * MOST + rank
    routed = slot[None, :] == lax.iota(jnp.int32, 8 * MOST)[:, None]
    src = jnp.max(jnp.where(routed, order[None, :], -8192), axis=1).astype(jnp.int32)
    frames = codes.reshape(9, count, SLAB).transpose(0, 2, 1)
    kept = lax.iota(jnp.int32, SLAB)[:, None] < lengths[None, :]
    frames = jnp.where(kept[None], frames, -1).reshape(9, SLAB * count)
    frames = jnp.pad(frames, ((0, 7), (0, 0)), constant_values=-1)
    w23 = jnp.concatenate([w2, w3[None]], axis=0)
    w56 = jnp.concatenate([w5, w6[None]], axis=0)
    vmem = pl.BlockSpec(memory_space=pltpu.VMEM)
    anywhere = pl.BlockSpec(memory_space=pl.ANY)
    V = pltpu.VMEM
    sems = 90
    return pl.pallas_call(
        kernel,
        out_shape=jax.ShapeDtypeStruct((1024, 384), BF),
        in_specs=[vmem, pl.BlockSpec(memory_space=pltpu.SMEM)] + [anywhere] * 6 + [vmem] * 4,
        out_specs=vmem,
        scratch_shapes=[
            V((4, 2, 16, 128), jnp.int32),
            V((9, 64, 1024), F32),
            V((64, 1536), F32),
            V((96, 384), F32),
            V((2, 48, 768), F32),
            V((48, 768), F32),
            V((4, 48, 384), F32),
            V((9, 128, 1024), BF),
            V((1152, 256), BF),
            V((256, 1024), BF),
            V((256, 1024), BF),
            V((256, 1024), BF),
            V((256, 1024), BF),
            V((256, 1024), BF),
            V((256, 1024), BF),
            V((256, 1024), F32),
            V((128, 1024), BF),
            V((128, 1024), BF),
            V((4, 2, 2, 64, 1536), BF),
            V((4, 2, 2, 96, 1536), BF),
            V((8, 4, 2, 2, 48, 768), BF),
            V((4, 2, 2, 48, 768), BF),
            V((2, 4, 4, 2, 48, 384), BF),
            V((128, 1024), BF),
            V((128, 1536), BF),
            V((16, 2, 8, 768), F32),
            V((8 * (2 * PAD1 + 32), 768), BF),
            V((8 * (2 * PAD1 + 34), 768), BF),
            V((256, 768), F32),
            V((256, 768), BF),
            V((256, 768), BF),
            V((32, 2, 8, 384), F32),
            V((8 * (2 * PAD2 + 64), 384), BF),
            V((8 * (2 * PAD2 + 66), 384), BF),
            V((512, 384), BF),
            V((512, 384), BF),
            V((8, 128, 384), BF),
            pltpu.SemaphoreType.DMA((sems,)),
            pltpu.SemaphoreType.DMA((sems,)),
            pltpu.SemaphoreType.DMA((6,)),
        ],
        compiler_params=pltpu.CompilerParams(
            collective_id=0, has_side_effects=True, vmem_limit_bytes=60 * 1024 * 1024
        ),
        cost_estimate=pl.CostEstimate(flops=7_400_000_000, bytes_accessed=8_000_000, transcendentals=0),
    )(frames, src, codebook, w0, w1, w23, w4, w56, a0[None], a1[None], a2[None], a3[None])


def solution(mesh):
    return jax.shard_map(
        body,
        mesh=mesh,
        in_specs=(
            P(None, ("fsdp", "dp")),
            P(("fsdp", "dp")),
            P(("fsdp", "dp"), None),
            P(None, "fsdp", None),
            P("fsdp", None),
            P(),
            P("fsdp", None),
            P(),
            P(None, "fsdp", None),
            P("fsdp", None),
            P(),
            P("fsdp", None),
            P(),
            P(None, "fsdp", None),
            P("fsdp", None),
        ),
        out_specs=P(("fsdp", "dp"), None),
        check_vma=False,
    )
```

time: 665 us -> 130 us (0.20); the launches traced: 655 us -> 130 us
  waiting for transfers between devices: 378 us -> 0 us
  matrix products: 174 us -> 0 us
  Pallas kernels: 0 us -> 114 us
  blocking collectives: 46.9 us -> 0 us
  other arithmetic: 22.2 us -> 6.53 us
  between operations: 14.3 us -> 0.05 us
  starting transfers between devices: 10.4 us -> 0 us
    all_gather x6 -> x0, waiting for transfers between devices: 266 us -> none  [project_latent(): lax.all_gather(shards[index], 'fsdp', axis=1, tiled=True)]
    dot_general x25 -> x0, matrix products: 174 us -> none  [the longest x9 104 us: dequantize(): jnp.dot(onehot, table[level], preferred_element_type=jnp.float32)]
    pallas_call x0 -> x1, Pallas kernels: none -> 114 us  [body(): pl.pallas_call(kernel, out_shape=jax.ShapeDtypeStruct((1024, 384), BF), i...]
    reduce_scatter x1 -> x0, waiting for transfers between devices: 108 us -> none  [dequantize(): return lax.psum_scatter(total, 'fsdp', scatter_dimension=0, tiled=True)]
    all_gather x2 -> x0, blocking collectives: 46.9 us -> none  [the longest x1 26.6 us: dequantize(): everyone = lax.all_gather(codes, 'fsdp', axis=1, tiled=True)]
    convert_element_type x10 -> x0, other arithmetic: 17 us -> none  [the longest x2 10.9 us: residual_stack_unit(): active_frames = snake(upper_bound, snake_frequency).astype(brain_float)]
    all_to_all x2 -> x0, starting transfers between devices: 10.1 us -> none  [the longest x1 6.88 us: body(): lax.all_to_all(send_codes, 'dp', split_axis=1, concat_axis=1, tiled=True)]
  transfers between devices with their start and end apart: 9 -> 0, of which waited for: 8 -> 0; matrix products, arithmetic and copies ran while one was open for 11% -> 0% of each run, Pallas kernels for 0% -> 0%
where the time goes in v1:
time: 130 us
  Pallas kernels  114 us (88%)
  local copies, waits for them, and re-layouts  8.73 us (7%)
  other arithmetic  6.53 us (5%)
    pallas_call x1, Pallas kernels, body(): pl.pallas_call(kernel, out_shape=jax.ShapeDtypeStruct((1024, 384), BF), i...  114 us

profile of v1, /device:TPU:1, one launch (start us, length us, event | category | flops | bytes accessed | tf_op | source)
XLA Modules:
  0.0 129.6 jit_solution(3252869686666552302)
XLA Ops:
  0.0 0.0 copy-start
  0.0 0.9 convert_reduce_fusion
  0.9 0.7 multiply_add_fusion
  1.6 0.6 select_reduce_fusion.src_ref
  2.2 1.3 broadcast_in_dim.59.a3_ref
  3.4 0.7 iota_compare_fusion
  4.1 1.3 broadcast_in_dim.57.a1_ref
  5.4 1.3 broadcast_in_dim.58.a2_ref
  6.6 1.3 broadcast_in_dim.56.a0_ref
  7.9 0.8 reshape.36
  8.7 0.1 copy.18
  8.8 0.1 reshape.37
  8.9 0.6 pad.4.codes_ref
  9.5 1.7 %pad_maximum_fusion.1.w56_hbm = f32[8,24,384]{2,1,0:T(8,128)} fusion(f32[1,24,384]{2,1,0:T(8,128)} %bitcast.7, f32[7,24,384]{2,1,0:T(8,128)} %param.28), kind=kLoop, calls=%fused_computation.1 | loop fusion | flops 73728 | bytes 589824 | tf_op jit(solution)/shard_map/concatenate | solution.py:470
  11.2 0.0 copy-done
  11.2 2.0 %pad_maximum_fusion.w23_hbm = f32[8,48,768]{2,1,0:T(8,128)} fusion(f32[1,48,768]{2,1,0:T(8,128)} %bitcast.6, f32[7,48,768]{2,1,0:T(8,128)S(1)} %copy-done), kind=kLoop, calls=%fused_computation | loop fusion | flops 294912 | bytes 2359296 | tf_op jit(solution)/shard_map/concatenate | solution.py:469
  13.2 114.3 %shard_map.145 = bf16[1024,384]{1,0:T(8,128)(2,1)} custom-call(s32[16,128]{1,0:T(8,128)} %pad.4.codes_ref, s32[16]{0:T(128)} %select_reduce_fusion.src_ref, f32[9,64,1024]{2,1,0:T(8,128)} %cb_hbm.1, f32[64,1536]{1,0:T(8,128)} %w0_hbm.1, f32[96,1536]{1,0:T(8,128)} %w1_hbm.1, f32[8,48,768]{2,1,0:T(8,128)} %pad_maximum_fusion.w23_hbm, f32[48,768]{1,0:T(8,128)} %w4_hbm.1, ...), custom_call_target="tpu_custom_call" | custom-call | flops 7400000000 | bytes 8000000 | tf_op jit(solution)/shard_map/pallas_call | solution.py:475
  127.5 2.1 %copy.20 = bf16[1024,384]{1,0:T(8,128)(2,1)} copy(bf16[1024,384]{1,0:T(8,128)(2,1)} %shard_map.145) | data formatting | bytes 1572864
  (1 shorter events, 0.0 us)
Async XLA Ops:
  0.0 11.2 %copy-start = (f32[7,48,768]{2,1,0:T(8,128)S(1)}, f32[7,48,768]{2,1,0:T(8,128)}, u32[]{:S(2)}) copy-start(f32[7,48,768]{2,1,0:T(8,128)} %param.23) | copy-start | bytes 3096580

commit v2 on v1

v2 whole, which is shorter than its diff:
```python
import jax
import jax.numpy as jnp
from jax import lax
from jax.experimental import pallas as pl
from jax.experimental.pallas import tpu as pltpu
from jax.sharding import PartitionSpec as P

SLAB = 16
MOST = 2
BF = jnp.bfloat16
F32 = jnp.float32
POLY = (
    9.869604311819561,
    -32.46967117891694,
    42.72719645855932,
    -30.101466599015037,
    13.05010051862992,
    -3.3565928630444257,
)
INV_PI = 0.3183098861837907
PAD1 = 8
PAD2 = 26


def snake(value, freq):
    turns = value * (freq * INV_PI)
    frac = turns - jnp.round(turns)
    u = frac * frac
    poly = jnp.full_like(u, POLY[-1])
    for coef in POLY[-2::-1]:
        poly = poly * u + coef
    return value + (poly * u) * (1.0 / freq)


def dot(left, right):
    return jnp.dot(left, right, preferred_element_type=F32)


class Links:
    def __init__(self, send_sems, recv_sems):
        self.send_sems, self.recv_sems, self.used, self.sent = send_sems, recv_sems, 0, []

    def new(self):
        self.used += 1
        return self.used - 1

    def copy(self, src, dst, dev, number):
        return pltpu.make_async_remote_copy(
            src_ref=src,
            dst_ref=dst,
            send_sem=self.send_sems.at[number],
            recv_sem=self.recv_sems.at[number],
            device_id=dev,
            device_id_type=pl.DeviceIdType.MESH,
        )

    def send(self, src, dev, number, dst=None):
        copy = self.copy(src, src if dst is None else dst, dev, number)
        copy.start()
        self.sent.append(copy)

    def wait(self, region, dev, number):
        self.copy(region, region, dev, number).wait_recv()


def kernel(
    codes_ref, lens_ref, owner_ref, cb_hbm, w0_hbm, a0_ref, w1_hbm, a1_ref, w2_hbm, w3_hbm, a2_ref, w4_hbm, a3_ref, w5_hbm, w6_hbm,
    out_ref,
    codes_all, cbf, w0f, w1f, wzf, whf, w4f, s56, table, onehot,
    fwd_out, fwd_in, far_out, far_in, sum_out, sum_in, keep, ypart_out, ypart_in,
    w0b, w1b, w23b, w4b, w56b,
    lat, lift1, up1, act_a1, act_b1, acc1, sec1, lift2, up2, act_a2, act_b2, sec2, block2, outbuf,
    send_sems, recv_sems, local_sems,
):
    f = lax.axis_index("fsdp")
    d = lax.axis_index("dp")
    x, yh, c = lax.div(f, 4), lax.rem(lax.div(f, 2), 2), lax.rem(f, 2)
    yl, z = lax.div(d, 4), lax.rem(d, 4)
    g = x * 2 + yh

    def dev(x_, yh_, yl_, z_, c_):
        return {"fsdp": (x_ * 2 + yh_) * 2 + c_, "dp": yl_ * 4 + z_}

    def plus(value, step):
        return lax.rem(value + step, 4)

    xp, xm, x2 = plus(x, 1), plus(x, 3), plus(x, 2)
    zp, zm, z2 = plus(z, 1), plus(z, 3), plus(z, 2)
    xs, xr = plus(x, 1 + 2 * c), plus(x, 3 + 2 * c)
    oyh = 1 - yh
    oyl = 1 - yl

    def at_x(xt):
        return dev(xt, yh, yl, z, c)

    def at_z(zt):
        return dev(x, yh, yl, zt, c)

    at_y = dev(x, oyh, oyl, z, c)
    at_b = dev(x, yh, oyl, z, c)
    sib = dev(x, yh, yl, z, 1 - c)
    links = Links(send_sems, recv_sems)
    local_count = [0]

    def load(src, dst):
        copy = pltpu.make_async_copy(src, dst, local_sems.at[local_count[0]])
        local_count[0] += 1
        copy.start()
        return copy

    zcols = pl.ds(pl.multiple_of(z * 384, 384), 384)
    ld_w1 = load(w1_hbm.at[:, zcols], w1f)
    ld_w0 = load(w0_hbm, w0f)
    ld_cb = load(cb_hbm, cbf)
    ld_wz = load(w2_hbm.at[z], wzf)
    ld_wh = load(w2_hbm.at[pl.ds(4, 3)], whf.at[pl.ds(0, 3)])
    ld_w3 = load(w3_hbm, whf.at[3])
    ld_w4 = load(w4_hbm, w4f)
    own24 = pl.ds(pl.multiple_of(c * 24, 8), 24)
    s56_own = s56.at[own24]
    own_last = (c == 1) & (z == 3)
    sib_last = (c == 0) & (z == 3)
    ld_56 = pltpu.make_async_copy(w6_hbm, s56_own, local_sems.at[7])

    @pl.when(own_last)
    def _():
        ld_56.start()

    @pl.when(jnp.logical_not(own_last))
    def _():
        pltpu.make_async_copy(w5_hbm.at[lax.rem(4 * c + z, 7)], s56_own, local_sems.at[7]).start()

    lane = lax.broadcasted_iota(jnp.int32, (9, 128), 1)
    room = jnp.zeros((9, 128), jnp.int32)
    for slab in range(8):
        room = jnp.where(lax.div(lane, SLAB) == slab, lens_ref[slab], room)
    codes_all[x, yh] = jnp.where(lax.rem(lane, SLAB) < room, codes_ref[...], -1)

    mates = []
    for step in range(4):
        if step:
            mates.append(at_x(plus(x, step)))
        mates.append(dev(plus(x, step), oyh, oyl, z, c))
    owners = [lax.rem(d + step, 8) for step in range(1, 8)]
    barrier = pltpu.get_barrier_semaphore()
    peers = mates + [sib] + [{"fsdp": f, "dp": o} for o in owners]
    for peer in peers:
        pl.semaphore_signal(barrier, inc=1, device_id=peer, device_id_type=pl.DeviceIdType.MESH)
    pl.semaphore_wait(barrier, len(peers))

    class Quarter:
        def __init__(self, block, row, full):
            self.block, self.row, self.full = block, row, full
            self.ids = [links.new() for _ in range(17)]

        def start(self):
            for number, place in zip(self.ids[:4], (at_x(xp), at_x(xm), at_x(x2), at_y)):
                links.send(self.block(z, x, yh), place, number)

        def x_in(self):
            for k, xt in enumerate((xm, xp, x2)):
                links.wait(self.block(z, xt, yh), at_x(xt), self.ids[k])
                links.send(self.block(z, xt, yh), at_y, self.ids[4 + k])
            links.send(self.row(z, yh), at_z(zp), self.ids[7])
            links.send(self.row(z, yh), at_z(zm), self.ids[8])

        def y_in(self):
            for k, xt in enumerate((x, xm, xp, x2)):
                links.wait(self.block(z, xt, oyh), at_y, self.ids[3 + k])
            links.send(self.row(z, oyh), at_z(zp), self.ids[9])
            links.send(self.row(z, oyh), at_z(zm), self.ids[10])
            links.send(self.full(z), sib, self.ids[13])

        def pass_own(self):
            links.wait(self.row(zm, yh), at_z(zm), self.ids[7])
            links.send(self.row(zm, yh), at_z(zp), self.ids[11])
            links.wait(self.row(zp, yh), at_z(zp), self.ids[8])

        def pass_other(self):
            links.wait(self.row(zp, oyh), at_z(zp), self.ids[10])
            links.send(self.row(zp, oyh), at_z(zm), self.ids[12])
            links.wait(self.row(zm, oyh), at_z(zm), self.ids[9])
            links.send(self.full(zp), sib, self.ids[14])
            links.send(self.full(zm), sib, self.ids[15])

        def finish(self):
            links.wait(self.row(z2, yh), at_z(zm), self.ids[11])
            links.wait(self.row(z2, oyh), at_z(zp), self.ids[12])
            links.send(self.full(z2), sib, self.ids[16])

        def done(self):
            for number, zt in zip(self.ids[13:], (z, zp, zm, z2)):
                links.wait(self.full(zt), sib, number)

    class Plain:
        def __init__(self, block, pair):
            self.block, self.pair = block, pair
            self.ids = [links.new() for _ in range(11)]

        def start(self):
            for number, place in zip(self.ids[:3], (at_y, at_x(xp), at_x(xm))):
                links.send(self.block(x, yh), place, number)

        def to_x(self):
            links.wait(self.block(x, oyh), at_y, self.ids[0])
            links.send(self.block(x, oyh), at_x(xp), self.ids[3])
            links.send(self.block(x, oyh), at_x(xm), self.ids[4])
            links.send(self.pair(x), sib, self.ids[7])

        def pass_own(self):
            links.wait(self.block(xm, yh), at_x(xm), self.ids[1])
            links.send(self.block(xm, yh), at_x(xp), self.ids[5])
            links.wait(self.block(xp, yh), at_x(xp), self.ids[2])

        def pass_other(self):
            links.wait(self.block(xp, oyh), at_x(xp), self.ids[4])
            links.send(self.block(xp, oyh), at_x(xm), self.ids[6])
            links.wait(self.block(xm, oyh), at_x(xm), self.ids[3])
            links.send(self.pair(xp), sib, self.ids[8])
            links.send(self.pair(xm), sib, self.ids[9])

        def finish(self):
            links.wait(self.block(x2, yh), at_x(xm), self.ids[5])
            links.wait(self.block(x2, oyh), at_x(xp), self.ids[6])
            links.send(self.pair(x2), sib, self.ids[10])

        def done(self):
            for number, xt in zip(self.ids[7:], (x, xp, xm, x2)):
                links.wait(self.pair(xt), sib, number)

    class Half:
        def __init__(self, block, pair, full):
            self.block, self.pair, self.full = block, pair, full
            self.ids = [links.new() for _ in range(13)]

        def start(self):
            links.send(self.block(oyl, x, yh), at_y, self.ids[0])
            links.send(self.block(yl, x, yh), at_x(xp), self.ids[1])
            links.send(self.block(yl, x, yh), at_x(xm), self.ids[2])

        def to_x(self):
            links.wait(self.block(yl, x, oyh), at_y, self.ids[0])
            links.send(self.block(yl, x, oyh), at_x(xp), self.ids[3])
            links.send(self.block(yl, x, oyh), at_x(xm), self.ids[4])
            links.send(self.block(yl, x, oyh), at_b, self.ids[7])

        def pass_own(self):
            links.wait(self.block(yl, xm, yh), at_x(xm), self.ids[1])
            links.send(self.block(yl, xm, yh), at_x(xp), self.ids[5])
            links.wait(self.block(yl, xp, yh), at_x(xp), self.ids[2])

        def pass_other(self):
            links.wait(self.block(yl, xp, oyh), at_x(xp), self.ids[4])
            links.send(self.block(yl, xp, oyh), at_x(xm), self.ids[6])
            links.wait(self.block(yl, xm, oyh), at_x(xm), self.ids[3])
            links.send(self.pair(yl, xp), at_b, self.ids[8])
            links.send(self.pair(yl, xm), at_b, self.ids[9])

        def finish(self):
            links.wait(self.block(yl, x2, yh), at_x(xm), self.ids[5])
            links.wait(self.block(yl, x2, oyh), at_x(xp), self.ids[6])
            links.send(self.pair(yl, x2), at_b, self.ids[10])
            links.send(self.full(yl), sib, self.ids[11])

        def b_in(self):
            links.wait(self.block(oyl, x, oyh), at_b, self.ids[7])
            for number, xt in zip(self.ids[8:11], (xp, xm, x2)):
                links.wait(self.pair(oyl, xt), at_b, number)
            links.send(self.full(oyl), sib, self.ids[12])

        def done(self):
            links.wait(self.full(yl), sib, self.ids[11])
            links.wait(self.full(oyl), sib, self.ids[12])

    def columns(zt):
        return pl.ds(pl.multiple_of(zt * 384, 384), 384)

    def pair_of_taps(t):
        return pl.ds(4 + 2 * t, 2)

    q1 = Quarter(
        lambda zt, xt, yt: w1b.at[xt, yt, c, :, columns(zt)],
        lambda zt, yt: w1b.at[:, yt, c, :, columns(zt)],
        lambda zt: w1b.at[:, :, c, :, columns(zt)],
    )
    qz = Quarter(
        lambda zt, xt, yt: w23b.at[zt, xt, yt, c],
        lambda zt, yt: w23b.at[zt, :, yt, c],
        lambda zt: w23b.at[zt, :, :, c],
    )
    q56 = Quarter(
        lambda zt, xt, yt: w56b.at[c, zt, xt, yt],
        lambda zt, yt: w56b.at[c, zt, :, yt],
        lambda zt: w56b.at[c, zt],
    )
    hh = Half(
        lambda t, xt, yt: w23b.at[pair_of_taps(t), xt, yt, c],
        lambda t, xt: w23b.at[pair_of_taps(t), xt, :, c],
        lambda t: w23b.at[pair_of_taps(t), :, :, c],
    )
    p0 = Plain(lambda xt, yt: w0b.at[xt, yt, c], lambda xt: w0b.at[xt, :, c])
    p4 = Plain(lambda xt, yt: w4b.at[xt, yt, c], lambda xt: w4b.at[xt, :, c])

    ld_w1.wait()
    w1b[x, yh, c, :, zcols] = w1f[...].astype(BF)
    q1.start()
    code_ids = [links.new() for _ in mates]
    for number, mate in zip(code_ids, mates):
        links.send(codes_all.at[x, yh], mate, number)
    ld_w0.wait()
    w0b[x, yh, c] = w0f[...].astype(BF)
    p0.start()

    ld_cb.wait()
    own64 = pl.ds(pl.multiple_of(c * 64, 64), 64)
    oth64 = pl.ds(pl.multiple_of((1 - c) * 64, 64), 64)
    for level in range(9):
        table[level, own64, :] = cbf[level].astype(BF)
    id_table = links.new()
    links.send(table.at[:, own64], sib, id_table)

    id_56 = links.new()
    to_56 = links.copy(w6_hbm, s56_own, sib, id_56)
    links.sent.append(to_56)

    @pl.when(sib_last)
    def _():
        to_56.start()

    @pl.when(jnp.logical_not(sib_last))
    def _():
        links.copy(w5_hbm.at[lax.rem(4 * (1 - c) + z, 7)], s56_own, sib, id_56).start()

    q1.x_in()
    ld_wz.wait()
    w23b[z, x, yh, c] = wzf[...].astype(BF)
    qz.start()

    for number, mate in zip(code_ids, mates):
        links.wait(codes_all.at[x, yh], mate, number)
    links.wait(table.at[:, oth64], sib, id_table)

    def partial(xt, put):
        place = lax.broadcasted_iota(jnp.int32, (128, 128), 0) + g * 128
        for yt in range(2):
            codes = codes_all[xt, yt]
            for level in range(9):
                hit = codes[level : level + 1, :] == place
                onehot[pl.ds(level * 128, 128), pl.ds(yt * 128, 128)] = jnp.where(hit, 1.0, 0.0).astype(BF)

        def tile(n, carry):
            cols = pl.ds(pl.multiple_of(n * 256, 256), 256)
            rows = table[:, :, cols].reshape(1152, 256)
            total = lax.dot_general(onehot[...], rows, (((0,), (0,)), ((), ())), preferred_element_type=F32)
            put(cols, total)
            return carry

        lax.fori_loop(0, 4, tile, 0)

    def into(ref):
        def put(cols, total):
            ref[:, cols] = total.astype(ref.dtype)

        return put

    id_fwd, id_far, id_sum, id_y = (links.new() for _ in range(4))
    partial(x2, into(fwd_out))
    links.send(fwd_out, at_x(xs), id_fwd, dst=fwd_in)
    partial(xr, into(far_out))
    links.send(far_out, at_x(xr), id_far, dst=far_in)
    q1.y_in()
    p0.to_x()
    qz.x_in()
    partial(xs, into(keep))
    links.wait(fwd_in, at_x(xr), id_fwd)
    sum_out[...] = (keep[...] + fwd_in[...].astype(F32)).astype(BF)
    links.send(sum_out, at_x(xs), id_sum, dst=sum_in)
    p0.pass_own()
    q1.pass_own()
    qz.y_in()
    ld_56.wait()
    links.wait(s56_own, sib, id_56)
    w56b[c, z, x, yh] = s56[...].astype(BF)
    q56.start()
    ld_wh.wait()
    ld_w3.wait()
    for k in range(4):
        w23b[4 + k, x, yh, c] = whf[k].astype(BF)
    hh.start()
    partial(x, into(keep))
    p0.pass_other()
    q1.pass_other()
    q56.x_in()
    ld_w4.wait()
    w4b[x, yh, c] = w4f[...].astype(BF)
    links.wait(far_in, at_x(xs), id_far)
    links.wait(sum_in, at_x(xr), id_sum)
    keep[...] += far_in[...].astype(F32) + sum_in[...].astype(F32)
    mine = pl.ds(pl.multiple_of(yh * 128, 128), 128)
    theirs = pl.ds(pl.multiple_of(oyh * 128, 128), 128)
    ypart_out[...] = keep[theirs, :].astype(BF)
    links.send(ypart_out, at_y, id_y, dst=ypart_in)
    p4.start()
    hh.to_x()
    qz.pass_own()
    q56.y_in()
    p0.finish()
    q1.finish()
    hh.pass_own()
    p4.to_x()
    links.wait(ypart_in, at_y, id_y)
    keep[mine, :] += ypart_in[...].astype(F32)
    row = lax.broadcasted_iota(jnp.int32, (128, 128), 0)
    place = lax.broadcasted_iota(jnp.int32, (128, 128), 1)
    order = jnp.where(place == lax.rem(row, 8) * SLAB + lax.div(row, 8), 1.0, 0.0).astype(BF)
    lat[...] = dot(order, keep[mine, :].astype(BF)).astype(BF)
    p0.done()

    def start_tile(n, carry):
        cols = pl.ds(pl.multiple_of(n * 256, 256), 256)
        total = dot(lat[...], w0b[:, :, :, :, cols].reshape(1024, 256))
        lift1[:, cols] = snake(total, a0_ref[cols].reshape(1, 256)).astype(BF)
        return carry

    lax.fori_loop(0, 6, start_tile, 0)
    qz.pass_other()
    hh.pass_other()
    q1.done()

    def up1_tile(n, carry):
        cols = pl.ds(pl.multiple_of(n * 256, 256), 256)
        total = dot(lift1[...], w1b[:, :, :, :, cols].reshape(1536, 256))
        phase, part = lax.div(n, 3), lax.rem(n, 3)
        up1[:, phase, :, pl.ds(pl.multiple_of(part * 256, 256), 256)] = total.reshape(16, 8, 256)
        return carry

    lax.fori_loop(0, 6, up1_tile, 0)
    p4.pass_own()
    q56.pass_own()
    hh.finish()
    p4.pass_other()

    act_a1[pl.ds(0, 8 * PAD1), :] = jnp.zeros((8 * PAD1, 768), BF)
    act_a1[pl.ds(8 * (PAD1 + 32), 8 * PAD1), :] = jnp.zeros((8 * PAD1, 768), BF)
    act_b1[pl.ds(0, 8 * PAD1), :] = jnp.zeros((8 * PAD1, 768), BF)
    act_b1[pl.ds(8 * (PAD1 + 34), 8 * PAD1), :] = jnp.zeros((8 * PAD1, 768), BF)

    def act1_tile(n, carry):
        cols = pl.ds(pl.multiple_of(n * 256, 256), 256)
        act = snake(up1[:, :, :, cols].reshape(256, 256), a1_ref[cols].reshape(1, 256))
        edge = jnp.zeros((8, 256), F32)
        act_a1[pl.ds(8 * PAD1, 256), cols] = act.astype(BF)
        act_b1[pl.ds(8 * PAD1, 272), cols] = jnp.concatenate([edge, act, edge], axis=0).astype(BF)
        return carry

    lax.fori_loop(0, 3, act1_tile, 0)
    qz.finish()
    hh.b_in()
    p4.finish()
    q56.pass_other()

    def conv1_tile(taps, n):
        cols = pl.ds(pl.multiple_of(n * 256, 256), 256)
        total = None
        for tap in taps:
            shift = 3 * (tap - 3)
            if shift % 2:
                window = act_b1[pl.ds(8 * (PAD1 + 1 + shift), 256), :]
            else:
                window = act_a1[pl.ds(8 * (PAD1 + shift), 256), :]
            term = dot(window, w23b[tap, :, :, :, :, cols].reshape(768, 256))
            total = term if total is None else total + term
        return cols, total

    def conv1_first(n, carry):
        cols, total = conv1_tile((0, 1, 2, 3), n)
        acc1[:, cols] = total
        return carry

    def conv1_rest(n, carry):
        cols, total = conv1_tile((4, 5, 6), n)
        sec1[:, cols] = snake(acc1[:, cols] + total, a1_ref[cols].reshape(1, 256)).astype(BF)
        return carry

    qz.done()
    lax.fori_loop(0, 3, conv1_first, 0)
    hh.done()
    lax.fori_loop(0, 3, conv1_rest, 0)

    def mix1_tile(n, carry):
        cols = pl.ds(pl.multiple_of(n * 256, 256), 256)
        total = dot(sec1[...], w23b[7, :, :, :, :, cols].reshape(768, 256))
        block = up1[:, :, :, cols].reshape(256, 256) + total
        lift2[:, cols] = snake(block, a2_ref[cols].reshape(1, 256)).astype(BF)
        return carry

    lax.fori_loop(0, 3, mix1_tile, 0)
    q56.finish()
    p4.done()

    def up2_tile(n, carry):
        rows = pl.ds(pl.multiple_of(n * 64, 64), 64)
        total = dot(lift2[rows, :], w4b[...].reshape(768, 768))
        for phase in range(2):
            up2[pl.ds(n * 8, 8), phase] = total[:, phase * 384 : (phase + 1) * 384].reshape(8, 8, 384)
        return carry

    lax.fori_loop(0, 4, up2_tile, 0)

    act_a2[pl.ds(0, 8 * PAD2), :] = jnp.zeros((8 * PAD2, 384), BF)
    act_a2[pl.ds(8 * (PAD2 + 64), 8 * PAD2), :] = jnp.zeros((8 * PAD2, 384), BF)
    act_b2[pl.ds(0, 8 * PAD2), :] = jnp.zeros((8 * PAD2, 384), BF)
    act_b2[pl.ds(8 * (PAD2 + 66), 8 * PAD2), :] = jnp.zeros((8 * PAD2, 384), BF)

    def act2_tile(n, carry):
        cols = pl.ds(pl.multiple_of(n * 128, 128), 128)
        act = snake(up2[:, :, :, cols].reshape(512, 128), a3_ref[cols].reshape(1, 128))
        edge = jnp.zeros((8, 128), F32)
        act_a2[pl.ds(8 * PAD2, 512), cols] = act.astype(BF)
        act_b2[pl.ds(8 * PAD2, 528), cols] = jnp.concatenate([edge, act, edge], axis=0).astype(BF)
        return carry

    lax.fori_loop(0, 3, act2_tile, 0)
    q56.done()

    def conv2_tile(n, carry):
        start = n * 128
        total = None
        for tap in range(7):
            shift = 9 * (tap - 3)
            if shift % 2:
                window = act_b2[pl.ds(pl.multiple_of(8 * (PAD2 + 1 + shift) + start, 16), 128), :]
            else:
                window = act_a2[pl.ds(pl.multiple_of(8 * (PAD2 + shift) + start, 16), 128), :]
            term = dot(window, w56b[tap // 4, tap % 4].reshape(384, 384))
            total = term if total is None else total + term
        second = snake(total, a3_ref[...].reshape(1, 384)).astype(BF)
        block = up2[pl.ds(n * 8, 8)].reshape(128, 384) + dot(second, w56b[1, 3].reshape(384, 384))
        block2[pl.ds(pl.multiple_of(start, 128), 128), :] = block.astype(BF)
        return carry

    lax.fori_loop(0, 4, conv2_tile, 0)

    dest = [owner_ref[slab, 0] for slab in range(8)]
    slots = []
    for slab in range(8):
        rank = jnp.int32(0)
        for before in range(slab):
            rank = rank + jnp.where(dest[before] == dest[slab], 1, 0)
        slots.append(dest[slab] * MOST + rank)
    lane = lax.broadcasted_iota(jnp.int32, (64, 512), 1)
    named = jnp.zeros((64, 512), jnp.int32)
    for slab in range(8):
        named = jnp.where(lax.rem(lane, 8) == slab, slots[slab], named)
    named = jnp.where(lax.div(lane, 8) == lax.broadcasted_iota(jnp.int32, (64, 512), 0), named, -1)
    for owner in range(8):
        pick = jnp.concatenate(
            [jnp.where(named == owner * MOST + r, 1.0, 0.0).astype(BF) for r in range(MOST)], axis=0
        )
        outbuf[owner] = dot(pick, block2[...]).astype(BF)
    out_ids = [links.new() for _ in owners]
    here = pl.ds(pl.multiple_of(d * 128, 128), 128)
    for number, o in zip(out_ids, owners):
        links.send(outbuf.at[o], {"fsdp": f, "dp": o}, number, dst=out_ref.at[here])
    out_ref[here, :] = outbuf[d]
    for number in out_ids:
        links.wait(out_ref.at[here], sib, number)
    for copy in links.sent:
        copy.wait_send()


def body(codes, lengths, owner, *rest):
    vmem = pl.BlockSpec(memory_space=pltpu.VMEM)
    smem = pl.BlockSpec(memory_space=pltpu.SMEM)
    hbm = pl.BlockSpec(memory_space=pl.ANY)
    V = pltpu.VMEM
    sems = 150
    return pl.pallas_call(
        kernel,
        out_shape=jax.ShapeDtypeStruct((1024, 384), BF),
        in_specs=[vmem, smem, smem, hbm, hbm, vmem, hbm, vmem, hbm, hbm, vmem, hbm, vmem, hbm, hbm],
        out_specs=vmem,
        scratch_shapes=[
            V((4, 2, 9, 128), jnp.int32),
            V((9, 64, 1024), F32),
            V((64, 1536), F32),
            V((96, 384), F32),
            V((48, 768), F32),
            V((4, 48, 768), F32),
            V((48, 768), F32),
            V((48, 384), F32),
            V((9, 128, 1024), BF),
            V((1152, 256), BF),
            V((256, 1024), BF),
            V((256, 1024), BF),
            V((256, 1024), BF),
            V((256, 1024), BF),
            V((256, 1024), BF),
            V((256, 1024), BF),
            V((256, 1024), F32),
            V((128, 1024), BF),
            V((128, 1024), BF),
            V((4, 2, 2, 64, 1536), BF),
            V((4, 2, 2, 96, 1536), BF),
            V((8, 4, 2, 2, 48, 768), BF),
            V((4, 2, 2, 48, 768), BF),
            V((2, 4, 4, 2, 48, 384), BF),
            V((128, 1024), BF),
            V((128, 1536), BF),
            V((16, 2, 8, 768), F32),
            V((8 * (2 * PAD1 + 32), 768), BF),
            V((8 * (2 * PAD1 + 34), 768), BF),
            V((256, 768), F32),
            V((256, 768), BF),
            V((256, 768), BF),
            V((32, 2, 8, 384), F32),
            V((8 * (2 * PAD2 + 64), 384), BF),
            V((8 * (2 * PAD2 + 66), 384), BF),
            V((512, 384), BF),
            V((512, 384), BF),
            V((8, 128, 384), BF),
            pltpu.SemaphoreType.DMA((sems,)),
            pltpu.SemaphoreType.DMA((sems,)),
            pltpu.SemaphoreType.DMA((8,)),
        ],
        compiler_params=pltpu.CompilerParams(
            collective_id=0, has_side_effects=True, vmem_limit_bytes=60 * 1024 * 1024
        ),
        cost_estimate=pl.CostEstimate(flops=7_400_000_000, bytes_accessed=8_000_000, transcendentals=0),
    )(codes, lengths, owner, *rest)


def solution(mesh):
    return jax.shard_map(
        body,
        mesh=mesh,
        in_specs=(
            P(None, ("fsdp", "dp")),
            P(("fsdp", "dp")),
            P(("fsdp", "dp"), None),
            P(None, "fsdp", None),
            P("fsdp", None),
            P(),
            P("fsdp", None),
            P(),
            P(None, "fsdp", None),
            P("fsdp", None),
            P(),
            P("fsdp", None),
            P(),
            P(None, "fsdp", None),
            P("fsdp", None),
        ),
        out_specs=P(("fsdp", "dp"), None),
        check_vma=False,
    )
```

time: 130 us -> 110 us (0.85)
  Pallas kernels: 114 us -> 105 us
  other arithmetic: 6.53 us -> 0 us
  local copies, waits for them, and re-layouts: 8.73 us -> 3.41 us
    pallas_call x1, Pallas kernels: 114 us -> 105 us  [body(): pl.pallas_call(kernel, out_shape=jax.ShapeDtypeStruct((1024, 384), BF), i...]
    broadcast_in_dim x4 -> x0, local copies, waits for them, and re-layouts: 5.09 us -> none  [the longest x1 1.28 us: body(): a0[None]]
    concatenate x2 -> x0, other arithmetic: 3.7 us -> none  [the longest x1 1.99 us: body(): w23 = jnp.concatenate([w2, w3[None]], axis=0)]
    unnamed x3 -> x2, local copies, waits for them, and re-layouts: 2.1 us -> 3.41 us
where the time goes in v2:
time: 110 us; the launch traced here: 109 us
  Pallas kernels  105 us (95%)
  local copies, waits for them, and re-layouts  3.41 us (3%)
    pallas_call x1, Pallas kernels, body(): pl.pallas_call(kernel, out_shape=jax.ShapeDtypeStruct((1024, 384), BF), i...  105 us
    unnamed x2, local copies, waits for them, and re-layouts  3.41 us

profile of v2, /device:TPU:1, one launch (start us, length us, event | category | flops | bytes accessed | tf_op | source)
XLA Modules:
  0.0 108.8 jit_solution(6759903205509296873)
XLA Ops:
  0.0 1.3 %copy.16.owner_ref = s32[8,1]{1,0:T(8,128)} copy(s32[8,1]{0,1:T(1,128)} %param.17) | data formatting | bytes 64 | tf_op args[2]
  1.3 105.3 %shard_map.145 = bf16[1024,384]{1,0:T(8,128)(2,1)} custom-call(s32[9,128]{1,0:T(8,128)} %codes_ref.1, s32[8]{0:T(128)} %lens_ref.1, s32[8,1]{1,0:T(8,128)} %copy.16.owner_ref, f32[9,64,1024]{2,1,0:T(8,128)} %cb_hbm.1, f32[64,1536]{1,0:T(8,128)} %w0_hbm.1, f32[1536]{0:T(1024)} %a0_ref.1, f32[96,1536]{1,0:T(8,128)} %w1_hbm.1, f32[768]{0:T(1024)} %a1_ref.1, ...), custom_call_target="tpu_custom_call" | custom-call | flops 7400000000 | bytes 8000000 | tf_op jit(solution)/shard_map/pallas_call | solution.py:578
  106.7 2.1 %copy.18 = bf16[1024,384]{1,0:T(8,128)(2,1)} copy(bf16[1024,384]{1,0:T(8,128)(2,1)} %shard_map.145) | data formatting | bytes 1572864

commit v3 on v2

--- a/solution.py
+++ b/solution.py
@@ -69,7 +69,7 @@
     codes_all, cbf, w0f, w1f, wzf, whf, w4f, s56, table, onehot,
     fwd_out, fwd_in, far_out, far_in, sum_out, sum_in, keep, ypart_out, ypart_in,
     w0b, w1b, w23b, w4b, w56b,
-    lat, lift1, up1, act_a1, act_b1, acc1, sec1, lift2, up2, act_a2, act_b2, sec2, block2, outbuf,
+    lat, lift1, up1, act_a1, act_b1, acc1, sec1, lift2, up2, act_a2, act_b2, pick, outbuf,
     send_sems, recv_sems, local_sems,
 ):
     f = lax.axis_index("fsdp")
@@ -301,15 +301,32 @@
     p0 = Plain(lambda xt, yt: w0b.at[xt, yt, c], lambda xt: w0b.at[xt, :, c])
     p4 = Plain(lambda xt, yt: w4b.at[xt, yt, c], lambda xt: w4b.at[xt, :, c])
 
+    code_ids = [links.new() for _ in mates]
+    for number, mate in zip(code_ids, mates):
+        links.send(codes_all.at[x, yh], mate, number)
+
+    id_56 = links.new()
+    to_56 = links.copy(w6_hbm, s56_own, sib, id_56)
+    links.sent.append(to_56)
+
+    @pl.when(sib_last)
+    def _():
+        to_56.start()
+
+    @pl.when(jnp.logical_not(sib_last))
+    def _():
+        links.copy(w5_hbm.at[lax.rem(4 * (1 - c) + z, 7)], s56_own, sib, id_56).start()
+
     ld_w1.wait()
     w1b[x, yh, c, :, zcols] = w1f[...].astype(BF)
     q1.start()
-    code_ids = [links.new() for _ in mates]
-    for number, mate in zip(code_ids, mates):
-        links.send(codes_all.at[x, yh], mate, number)
-    ld_w0.wait()
-    w0b[x, yh, c] = w0f[...].astype(BF)
-    p0.start()
+    ld_wz.wait()
+    w23b[z, x, yh, c] = wzf[...].astype(BF)
+    qz.start()
+    ld_56.wait()
+    links.wait(s56_own, sib, id_56)
+    w56b[c, z, x, yh] = s56[...].astype(BF)
+    q56.start()
 
     ld_cb.wait()
     own64 = pl.ds(pl.multiple_of(c * 64, 64), 64)
@@ -318,23 +335,12 @@
         table[level, own64, :] = cbf[level].astype(BF)
     id_table = links.new()
     links.send(table.at[:, own64], sib, id_table)
-
-    id_56 = links.new()
-    to_56 = links.copy(w6_hbm, s56_own, sib, id_56)
-    links.sent.append(to_56)
-
-    @pl.when(sib_last)
-    def _():
-        to_56.start()
-
-    @pl.when(jnp.logical_not(sib_last))
-    def _():
-        links.copy(w5_hbm.at[lax.rem(4 * (1 - c) + z, 7)], s56_own, sib, id_56).start()
-
     q1.x_in()
-    ld_wz.wait()
-    w23b[z, x, yh, c] = wzf[...].astype(BF)
-    qz.start()
+    ld_wh.wait()
+    ld_w3.wait()
+    for k in range(4):
+        w23b[4 + k, x, yh, c] = whf[k].astype(BF)
+    hh.start()
 
     for number, mate in zip(code_ids, mates):
         links.wait(codes_all.at[x, yh], mate, number)
@@ -366,33 +372,33 @@
     id_fwd, id_far, id_sum, id_y = (links.new() for _ in range(4))
     partial(x2, into(fwd_out))
     links.send(fwd_out, at_x(xs), id_fwd, dst=fwd_in)
+    qz.x_in()
     partial(xr, into(far_out))
     links.send(far_out, at_x(xr), id_far, dst=far_in)
+    q56.x_in()
+    hh.to_x()
     q1.y_in()
-    p0.to_x()
-    qz.x_in()
+    ld_w0.wait()
+    w0b[x, yh, c] = w0f[...].astype(BF)
+    p0.start()
     partial(xs, into(keep))
+    q1.pass_own()
+    qz.y_in()
+    hh.pass_own()
+    q56.y_in()
+    q1.pass_other()
+    hh.pass_other()
     links.wait(fwd_in, at_x(xr), id_fwd)
     sum_out[...] = (keep[...] + fwd_in[...].astype(F32)).astype(BF)
     links.send(sum_out, at_x(xs), id_sum, dst=sum_in)
+    partial(x, into(keep))
+    p0.to_x()
     p0.pass_own()
-    q1.pass_own()
-    qz.y_in()
-    ld_56.wait()
-    links.wait(s56_own, sib, id_56)
-    w56b[c, z, x, yh] = s56[...].astype(BF)
-    q56.start()
-    ld_wh.wait()
-    ld_w3.wait()
-    for k in range(4):
-        w23b[4 + k, x, yh, c] = whf[k].astype(BF)
-    hh.start()
-    partial(x, into(keep))
-    p0.pass_other()
-    q1.pass_other()
-    q56.x_in()
+    hh.finish()
     ld_w4.wait()
     w4b[x, yh, c] = w4f[...].astype(BF)
+    q1.finish()
+    qz.pass_own()
     links.wait(far_in, at_x(xs), id_far)
     links.wait(sum_in, at_x(xr), id_sum)
     keep[...] += far_in[...].astype(F32) + sum_in[...].astype(F32)
@@ -400,20 +406,18 @@
     theirs = pl.ds(pl.multiple_of(oyh * 128, 128), 128)
     ypart_out[...] = keep[theirs, :].astype(BF)
     links.send(ypart_out, at_y, id_y, dst=ypart_in)
+    p0.pass_other()
     p4.start()
-    hh.to_x()
-    qz.pass_own()
-    q56.y_in()
-    p0.finish()
-    q1.finish()
-    hh.pass_own()
-    p4.to_x()
+    qz.pass_other()
     links.wait(ypart_in, at_y, id_y)
     keep[mine, :] += ypart_in[...].astype(F32)
     row = lax.broadcasted_iota(jnp.int32, (128, 128), 0)
     place = lax.broadcasted_iota(jnp.int32, (128, 128), 1)
     order = jnp.where(place == lax.rem(row, 8) * SLAB + lax.div(row, 8), 1.0, 0.0).astype(BF)
     lat[...] = dot(order, keep[mine, :].astype(BF)).astype(BF)
+    p0.finish()
+    p4.to_x()
+    hh.b_in()
     p0.done()
 
     def start_tile(n, carry):
@@ -423,8 +427,7 @@
         return carry
 
     lax.fori_loop(0, 6, start_tile, 0)
-    qz.pass_other()
-    hh.pass_other()
+    q56.pass_own()
     q1.done()
 
     def up1_tile(n, carry):
@@ -436,8 +439,6 @@
 
     lax.fori_loop(0, 6, up1_tile, 0)
     p4.pass_own()
-    q56.pass_own()
-    hh.finish()
     p4.pass_other()
 
     act_a1[pl.ds(0, 8 * PAD1), :] = jnp.zeros((8 * PAD1, 768), BF)
@@ -455,9 +456,8 @@
 
     lax.fori_loop(0, 3, act1_tile, 0)
     qz.finish()
-    hh.b_in()
+    q56.pass_other()
     p4.finish()
-    q56.pass_other()
 
     def conv1_tile(taps, n):
         cols = pl.ds(pl.multiple_of(n * 256, 256), 256)
@@ -521,7 +521,26 @@
         return carry
 
     lax.fori_loop(0, 3, act2_tile, 0)
+
+    dest = [owner_ref[slab] for slab in range(8)]
+    lane = lax.broadcasted_iota(jnp.int32, (16, 128), 1)
+    named = jnp.zeros((16, 128), jnp.int32)
+    for slab in range(8):
+        rank = jnp.int32(0)
+        for before in range(slab):
+            rank = rank + jnp.where(dest[before] == dest[slab], 1, 0)
+        named = jnp.where(lax.rem(lane, 8) == slab, dest[slab] * MOST + rank, named)
+    named = jnp.where(lax.div(lane, 8) == lax.broadcasted_iota(jnp.int32, (16, 128), 0), named, -1)
+    for slot in range(8 * MOST):
+        pick[pl.ds(slot * 16, 16), :] = jnp.where(named == slot, 1.0, 0.0).astype(BF)
     q56.done()
+    out_base = links.used
+
+    def out_copy(n, k):
+        frames = pl.ds(pl.multiple_of(n * 16, 16), 16)
+        return links.copy(
+            outbuf.at[n, owners[k]], out_ref.at[d, :, frames], {"fsdp": f, "dp": owners[k]}, out_base + n * 7 + k
+        )
 
     def conv2_tile(n, carry):
         start = n * 128
@@ -536,35 +555,21 @@
             total = term if total is None else total + term
         second = snake(total, a3_ref[...].reshape(1, 384)).astype(BF)
         block = up2[pl.ds(n * 8, 8)].reshape(128, 384) + dot(second, w56b[1, 3].reshape(384, 384))
-        block2[pl.ds(pl.multiple_of(start, 128), 128), :] = block.astype(BF)
+        slots = dot(pick[...], block.astype(BF)).astype(BF)
+        outbuf[n] = slots.reshape(8, MOST, 16, 384)
+        for k in range(7):
+            out_copy(n, k).start()
+        out_ref[d, :, pl.ds(pl.multiple_of(n * 16, 16), 16)] = outbuf[n, d]
         return carry
 
     lax.fori_loop(0, 4, conv2_tile, 0)
 
-    dest = [owner_ref[slab, 0] for slab in range(8)]
-    slots = []
-    for slab in range(8):
-        rank = jnp.int32(0)
-        for before in range(slab):
-            rank = rank + jnp.where(dest[before] == dest[slab], 1, 0)
-        slots.append(dest[slab] * MOST + rank)
-    lane = lax.broadcasted_iota(jnp.int32, (64, 512), 1)
-    named = jnp.zeros((64, 512), jnp.int32)
-    for slab in range(8):
-        named = jnp.where(lax.rem(lane, 8) == slab, slots[slab], named)
-    named = jnp.where(lax.div(lane, 8) == lax.broadcasted_iota(jnp.int32, (64, 512), 0), named, -1)
-    for owner in range(8):
-        pick = jnp.concatenate(
-            [jnp.where(named == owner * MOST + r, 1.0, 0.0).astype(BF) for r in range(MOST)], axis=0
-        )
-        outbuf[owner] = dot(pick, block2[...]).astype(BF)
-    out_ids = [links.new() for _ in owners]
-    here = pl.ds(pl.multiple_of(d * 128, 128), 128)
-    for number, o in zip(out_ids, owners):
-        links.send(outbuf.at[o], {"fsdp": f, "dp": o}, number, dst=out_ref.at[here])
-    out_ref[here, :] = outbuf[d]
-    for number in out_ids:
-        links.wait(out_ref.at[here], sib, number)
+    def out_wait(n, carry):
+        for k in range(7):
+            out_copy(n, k).wait()
+        return carry
+
+    lax.fori_loop(0, 4, out_wait, 0)
     for copy in links.sent:
         copy.wait_send()
 
@@ -574,10 +579,10 @@
     smem = pl.BlockSpec(memory_space=pltpu.SMEM)
     hbm = pl.BlockSpec(memory_space=pl.ANY)
     V = pltpu.VMEM
-    sems = 150
+    sems = 170
     return pl.pallas_call(
         kernel,
-        out_shape=jax.ShapeDtypeStruct((1024, 384), BF),
+        out_shape=jax.ShapeDtypeStruct((8, MOST, 64, 384), BF),
         in_specs=[vmem, smem, smem, hbm, hbm, vmem, hbm, vmem, hbm, hbm, vmem, hbm, vmem, hbm, hbm],
         out_specs=vmem,
         scratch_shapes=[
@@ -616,9 +621,8 @@
             V((32, 2, 8, 384), F32),
             V((8 * (2 * PAD2 + 64), 384), BF),
             V((8 * (2 * PAD2 + 66), 384), BF),
-            V((512, 384), BF),
-            V((512, 384), BF),
-            V((8, 128, 384), BF),
+            V((256, 128), BF),
+            V((4, 8, MOST, 16, 384), BF),
             pltpu.SemaphoreType.DMA((sems,)),
             pltpu.SemaphoreType.DMA((sems,)),
             pltpu.SemaphoreType.DMA((8,)),
@@ -627,7 +631,7 @@
             collective_id=0, has_side_effects=True, vmem_limit_bytes=60 * 1024 * 1024
         ),
         cost_estimate=pl.CostEstimate(flops=7_400_000_000, bytes_accessed=8_000_000, transcendentals=0),
-    )(codes, lengths, owner, *rest)
+    )(codes, lengths, owner.reshape(8), *rest).reshape(1024, 384)
 
 
 def solution(mesh):

time: 110 us -> 94.8 us (0.86)
  Pallas kernels: 105 us -> 92.6 us
  local copies, waits for them, and re-layouts: 3.41 us -> 2.09 us
    pallas_call x1, Pallas kernels: 105 us -> 92.6 us  [body(): pl.pallas_call(kernel, out_shape=jax.ShapeDtypeStruct((8, MOST, 64, 384),...]
    unnamed x2 -> x1, local copies, waits for them, and re-layouts: 3.41 us -> 2.09 us
where the time goes in v3:
time: 94.8 us; the launch traced here: 94.7 us
  Pallas kernels  92.6 us (98%)
  local copies, waits for them, and re-layouts  2.09 us (2%)
    pallas_call x1, Pallas kernels, body(): pl.pallas_call(kernel, out_shape=jax.ShapeDtypeStruct((8, MOST, 64, 384),...  92.6 us
    unnamed x1, local copies, waits for them, and re-layouts  2.09 us

profile of v3, /device:TPU:1, one launch (start us, length us, event | category | flops | bytes accessed | tf_op | source)
XLA Modules:
  0.0 94.7 jit_solution(15821674923145590734)
XLA Ops:
  0.0 92.6 %shard_map.145 = bf16[8,2,64,384]{3,2,1,0:T(8,128)(2,1)} custom-call(s32[9,128]{1,0:T(8,128)} %codes_ref.1, s32[8]{0:T(128)} %lens_ref.1, s32[8]{0:T(128)} %bitcast.3, f32[9,64,1024]{2,1,0:T(8,128)} %cb_hbm.1, f32[64,1536]{1,0:T(8,128)} %w0_hbm.1, f32[1536]{0:T(1024)} %a0_ref.1, f32[96,1536]{1,0:T(8,128)} %w1_hbm.1, f32[768]{0:T(1024)} %a1_ref.1, ...), custom_call_target="tpu_custom_call" | custom-call | flops 7400000000 | bytes 8000000 | tf_op jit(solution)/shard_map/pallas_call | solution.py:583
  92.6 2.1 %copy.17 = bf16[1024,384]{1,0:T(8,128)(2,1)} copy(bf16[1024,384]{1,0:T(8,128)(2,1)} %bitcast.2) | data formatting | bytes 1572864

commit v4 on v3

--- a/solution.py
+++ b/solution.py
@@ -352,12 +352,12 @@
             codes = codes_all[xt, yt]
             for level in range(9):
                 hit = codes[level : level + 1, :] == place
-                onehot[pl.ds(level * 128, 128), pl.ds(yt * 128, 128)] = jnp.where(hit, 1.0, 0.0).astype(BF)
+                onehot[pl.ds(yt * 128, 128), pl.ds(level * 128, 128)] = jnp.where(hit, 1.0, 0.0).T.astype(BF)
 
         def tile(n, carry):
             cols = pl.ds(pl.multiple_of(n * 256, 256), 256)
             rows = table[:, :, cols].reshape(1152, 256)
-            total = lax.dot_general(onehot[...], rows, (((0,), (0,)), ((), ())), preferred_element_type=F32)
+            total = dot(onehot[...], rows)
             put(cols, total)
             return carry
 
@@ -378,19 +378,19 @@
     q56.x_in()
     hh.to_x()
     q1.y_in()
-    ld_w0.wait()
-    w0b[x, yh, c] = w0f[...].astype(BF)
-    p0.start()
     partial(xs, into(keep))
     q1.pass_own()
     qz.y_in()
+    links.wait(fwd_in, at_x(xr), id_fwd)
+    sum_out[...] = (keep[...] + fwd_in[...].astype(F32)).astype(BF)
+    links.send(sum_out, at_x(xs), id_sum, dst=sum_in)
     hh.pass_own()
     q56.y_in()
     q1.pass_other()
     hh.pass_other()
-    links.wait(fwd_in, at_x(xr), id_fwd)
-    sum_out[...] = (keep[...] + fwd_in[...].astype(F32)).astype(BF)
-    links.send(sum_out, at_x(xs), id_sum, dst=sum_in)
+    ld_w0.wait()
+    w0b[x, yh, c] = w0f[...].astype(BF)
+    p0.start()
     partial(x, into(keep))
     p0.to_x()
     p0.pass_own()
@@ -417,7 +417,6 @@
     lat[...] = dot(order, keep[mine, :].astype(BF)).astype(BF)
     p0.finish()
     p4.to_x()
-    hh.b_in()
     p0.done()
 
     def start_tile(n, carry):
@@ -438,6 +437,7 @@
         return carry
 
     lax.fori_loop(0, 6, up1_tile, 0)
+    hh.b_in()
     p4.pass_own()
     p4.pass_other()
 
@@ -499,13 +499,13 @@
     p4.done()
 
     def up2_tile(n, carry):
-        rows = pl.ds(pl.multiple_of(n * 64, 64), 64)
+        rows = pl.ds(pl.multiple_of(n * 128, 128), 128)
         total = dot(lift2[rows, :], w4b[...].reshape(768, 768))
         for phase in range(2):
-            up2[pl.ds(n * 8, 8), phase] = total[:, phase * 384 : (phase + 1) * 384].reshape(8, 8, 384)
-        return carry
-
-    lax.fori_loop(0, 4, up2_tile, 0)
+            up2[pl.ds(n * 16, 16), phase] = total[:, phase * 384 : (phase + 1) * 384].reshape(16, 8, 384)
+        return carry
+
+    lax.fori_loop(0, 2, up2_tile, 0)
 
     act_a2[pl.ds(0, 8 * PAD2), :] = jnp.zeros((8 * PAD2, 384), BF)
     act_a2[pl.ds(8 * (PAD2 + 64), 8 * PAD2), :] = jnp.zeros((8 * PAD2, 384), BF)
@@ -523,53 +523,58 @@
     lax.fori_loop(0, 3, act2_tile, 0)
 
     dest = [owner_ref[slab] for slab in range(8)]
-    lane = lax.broadcasted_iota(jnp.int32, (16, 128), 1)
-    named = jnp.zeros((16, 128), jnp.int32)
+    lane = lax.broadcasted_iota(jnp.int32, (32, 256), 1)
+    named = jnp.zeros((32, 256), jnp.int32)
     for slab in range(8):
         rank = jnp.int32(0)
         for before in range(slab):
             rank = rank + jnp.where(dest[before] == dest[slab], 1, 0)
         named = jnp.where(lax.rem(lane, 8) == slab, dest[slab] * MOST + rank, named)
-    named = jnp.where(lax.div(lane, 8) == lax.broadcasted_iota(jnp.int32, (16, 128), 0), named, -1)
+    named = jnp.where(lax.div(lane, 8) == lax.broadcasted_iota(jnp.int32, (32, 256), 0), named, -1)
     for slot in range(8 * MOST):
-        pick[pl.ds(slot * 16, 16), :] = jnp.where(named == slot, 1.0, 0.0).astype(BF)
+        pick[pl.ds(slot * 32, 32), :] = jnp.where(named == slot, 1.0, 0.0).astype(BF)
     q56.done()
     out_base = links.used
 
     def out_copy(n, k):
-        frames = pl.ds(pl.multiple_of(n * 16, 16), 16)
+        frames = pl.ds(pl.multiple_of(n * 32, 32), 32)
         return links.copy(
             outbuf.at[n, owners[k]], out_ref.at[d, :, frames], {"fsdp": f, "dp": owners[k]}, out_base + n * 7 + k
         )
 
+    def own_copy(n):
+        frames = pl.ds(pl.multiple_of(n * 32, 32), 32)
+        return pltpu.make_async_copy(outbuf.at[n, d], out_ref.at[d, :, frames], local_sems.at[8 + n])
+
     def conv2_tile(n, carry):
-        start = n * 128
+        start = n * 256
         total = None
         for tap in range(7):
             shift = 9 * (tap - 3)
             if shift % 2:
-                window = act_b2[pl.ds(pl.multiple_of(8 * (PAD2 + 1 + shift) + start, 16), 128), :]
+                window = act_b2[pl.ds(pl.multiple_of(8 * (PAD2 + 1 + shift) + start, 16), 256), :]
             else:
-                window = act_a2[pl.ds(pl.multiple_of(8 * (PAD2 + shift) + start, 16), 128), :]
+                window = act_a2[pl.ds(pl.multiple_of(8 * (PAD2 + shift) + start, 16), 256), :]
             term = dot(window, w56b[tap // 4, tap % 4].reshape(384, 384))
             total = term if total is None else total + term
         second = snake(total, a3_ref[...].reshape(1, 384)).astype(BF)
-        block = up2[pl.ds(n * 8, 8)].reshape(128, 384) + dot(second, w56b[1, 3].reshape(384, 384))
+        block = up2[pl.ds(n * 16, 16)].reshape(256, 384) + dot(second, w56b[1, 3].reshape(384, 384))
         slots = dot(pick[...], block.astype(BF)).astype(BF)
-        outbuf[n] = slots.reshape(8, MOST, 16, 384)
+        outbuf[n] = slots.reshape(8, MOST, 32, 384)
         for k in range(7):
             out_copy(n, k).start()
-        out_ref[d, :, pl.ds(pl.multiple_of(n * 16, 16), 16)] = outbuf[n, d]
-        return carry
-
-    lax.fori_loop(0, 4, conv2_tile, 0)
+        own_copy(n).start()
+        return carry
+
+    lax.fori_loop(0, 2, conv2_tile, 0)
 
     def out_wait(n, carry):
         for k in range(7):
             out_copy(n, k).wait()
-        return carry
-
-    lax.fori_loop(0, 4, out_wait, 0)
+        own_copy(n).wait()
+        return carry
+
+    lax.fori_loop(0, 2, out_wait, 0)
     for copy in links.sent:
         copy.wait_send()
 
@@ -584,7 +589,7 @@
         kernel,
         out_shape=jax.ShapeDtypeStruct((8, MOST, 64, 384), BF),
         in_specs=[vmem, smem, smem, hbm, hbm, vmem, hbm, vmem, hbm, hbm, vmem, hbm, vmem, hbm, hbm],
-        out_specs=vmem,
+        out_specs=hbm,
         scratch_shapes=[
             V((4, 2, 9, 128), jnp.int32),
             V((9, 64, 1024), F32),
@@ -595,7 +600,7 @@
             V((48, 768), F32),
             V((48, 384), F32),
             V((9, 128, 1024), BF),
-            V((1152, 256), BF),
+            V((256, 1152), BF),
             V((256, 1024), BF),
             V((256, 1024), BF),
             V((256, 1024), BF),
@@ -621,11 +626,11 @@
             V((32, 2, 8, 384), F32),
             V((8 * (2 * PAD2 + 64), 384), BF),
             V((8 * (2 * PAD2 + 66), 384), BF),
-            V((256, 128), BF),
-            V((4, 8, MOST, 16, 384), BF),
+            V((512, 256), BF),
+            V((2, 8, MOST, 32, 384), BF),
             pltpu.SemaphoreType.DMA((sems,)),
             pltpu.SemaphoreType.DMA((sems,)),
-            pltpu.SemaphoreType.DMA((8,)),
+            pltpu.SemaphoreType.DMA((10,)),
         ],
         compiler_params=pltpu.CompilerParams(
             collective_id=0, has_side_effects=True, vmem_limit_bytes=60 * 1024 * 1024

time: 94.8 us -> 93.8 us (0.989)
  Pallas kernels: 92.6 us -> 91.5 us
    pallas_call x1, Pallas kernels: 92.6 us -> 91.5 us  [body(): pl.pallas_call(kernel, out_shape=jax.ShapeDtypeStruct((8, MOST, 64, 384),...]
where the time goes in v4:
time: 93.8 us; the launch traced here: 93.6 us
  Pallas kernels  91.5 us (98%)
  local copies, waits for them, and re-layouts  2.09 us (2%)
    pallas_call x1, Pallas kernels, body(): pl.pallas_call(kernel, out_shape=jax.ShapeDtypeStruct((8, MOST, 64, 384),...  91.5 us
    unnamed x1, local copies, waits for them, and re-layouts  2.09 us

profile of v4, /device:TPU:1, one launch (start us, length us, event | category | flops | bytes accessed | tf_op | source)
XLA Modules:
  0.0 93.6 jit_solution(11281441538930985719)
XLA Ops:
  0.0 91.5 %shard_map.145 = bf16[8,2,64,384]{3,2,1,0:T(8,128)(2,1)} custom-call(s32[9,128]{1,0:T(8,128)} %codes_ref.1, s32[8]{0:T(128)} %lens_ref.1, s32[8]{0:T(128)} %bitcast.3, f32[9,64,1024]{2,1,0:T(8,128)} %cb_hbm.1, f32[64,1536]{1,0:T(8,128)} %w0_hbm.1, f32[1536]{0:T(1024)} %a0_ref.1, f32[96,1536]{1,0:T(8,128)} %w1_hbm.1, f32[768]{0:T(1024)} %a1_ref.1, ...), custom_call_target="tpu_custom_call" | custom-call | flops 7400000000 | bytes 8000000 | tf_op jit(solution)/shard_map/pallas_call | solution.py:588
  91.5 2.1 %copy.17 = bf16[1024,384]{1,0:T(8,128)(2,1)} copy(bf16[1024,384]{1,0:T(8,128)(2,1)} %bitcast.2) | data formatting | bytes 1572864
